TPU v7x, 256 devices: a whole 4x4x8 slice. The times are simulated.
256 devices in a mesh: aa: 16 (over y, x_lo, core), ba: 8 (over z), ao: 2 (over x_hi).
Axes of the slice: x: 4 (x_hi: 2, x_lo: 2; x = x_hi * 2 + x_lo), y: 4, z: 8, core: 2. Of those that a mesh axis runs over, the one named last changes fastest.
Arguments:
- integrals: float32 [1048576, 256], P(('aa', 'ba')), may hold values from -0.375 to 0.375
- amplitudes: float32 [2048, 512], P(('aa', 'ba'), 'ao'), may hold values from -6 to 6
- row_irrep: int32 [8192], P(('aa', 'ba')), may hold values from 0 to 7
- cd_irrep: int32 [16], replicated, may hold values from 0 to 7, as said below
- cd_order: int32 [2048], replicated, may hold values from 0 to 2047, each once
Outputs:
- ladder: float32 [1048576, 512], P(('aa', 'ba'), 'ao')
Inputs may be any that keep to these rules, and one draw needn't show every extreme that they name: cd_order is a permutation of 0 to 2047. `cd_irrep`: every label appears exactly twice.
All inputs are finite; a program needn't handle non-finite values.
Results may differ from a plain program's by a relative error of at most 0.00007.
Values sent between devices are 32-bit elements; how exact they have to be, the bound alone decides.
No kernel may reach another device: no remote copies, remote signals or barrier semaphores. Data moves between devices by JAX's collectives and lax.ppermute only.
A program may use at most 128 MiB of HBM per device.

v0:
```python
import jax
import jax.numpy as jnp
from jax import lax
from jax.sharding import PartitionSpec as P


def partner(block, axis, bit):
    count = lax.axis_size(axis)
    route = []
    for low in range(count):
        high = low | 1 << bit
        if high != low and high < count:
            route += [(low, high), (high, low)]
    return lax.ppermute(block, axis, route)


def on_device(integrals, amplitudes, row_irrep, cd_irrep, cd_order):
    block_size = integrals.shape[1] // 2
    irrep_count = cd_irrep.shape[0] // 2
    parity = (1 - 2 * lax.axis_index("ao")).astype(jnp.float32)
    gathered = lax.all_gather(amplitudes, ("aa", "ba"), axis=0, tiled=True)
    sorted_blocks = jnp.argsort(cd_irrep, stable=True).reshape(irrep_count, 2)
    offsets = jnp.arange(block_size, dtype=jnp.int32)
    columns = (sorted_blocks[:, :, None] * block_size + offsets[None, None, :]).reshape(-1)
    amp_rows = jnp.take(cd_order, columns)
    picked = jnp.take(gathered, amp_rows, axis=0).reshape(
        irrep_count, 2 * block_size, gathered.shape[1]
    )
    per_block = jnp.take(picked, row_irrep, axis=0)
    slab_blocks = integrals.reshape(-1, block_size, 2 * block_size)
    result = jnp.einsum(
        "nrk,nkq->nrq",
        slab_blocks,
        per_block,
        precision=lax.Precision.HIGHEST,
        preferred_element_type=jnp.float32,
    )
    result = result.reshape(integrals.shape[0], gathered.shape[1])
    partner_result = partner(result, "ao", 0)
    result = partner_result[:, ::-1] + parity * result
    return result


def solution(mesh):
    placed = (P(("aa", "ba"), None), P(("aa", "ba"), "ao"), P(("aa", "ba")), P(), P())
    return jax.shard_map(
        on_device, mesh=mesh, in_specs=placed, out_specs=P(("aa", "ba"), "ao"), check_vma=False
    )
```

profile of v0, /device:TPU:1, one launch (start us, length us, event | category | flops | bytes accessed | tf_op | source)
XLA Modules:
  0.0 674.5 jit_solution(4354440395884586186)
XLA Ops:
  6.5 0.0 copy-start
  6.5 0.0 copy-start.1
  6.5 0.0 all-gather.2.cloned.1.call-start
  6.5 0.7 all-gather.2.cloned.1.call-update
  7.3 1.9 sort.17
  9.2 0.1 mul.18
  9.3 0.1 fusion.5
  9.4 0.0 copy-done
  9.4 11.8 %gather_fusion = s32[2048]{0:T(1024)S(1)} fusion(s32[2048]{0:T(1024)S(1)} %copy-done, s32[2048]{0:T(1024)S(1)} %broadcast_clamp_fusion.1), kind=kCustom, calls=%fused_computation | custom fusion | bytes 24576 | tf_op jit(solution)/shard_map/jit(_take)/gather | solution.py:25
  21.2 0.0 copy-done.1
  21.3 348.0 %all-gather.2.cloned.1.call-done = f32[2048,256]{1,0:T(8,128)} async-done(((f32[16,256]{1,0:T(8,128)}), f32[2048,256]{1,0:T(8,128)}) %all-gather.2.cloned.1.call-update) | async-done | bytes 2097168 | tf_op jit(solution)/shard_map/all_gather | solution.py:21
  369.3 10.2 %gather_fusion.1 = f32[2048,256]{1,0:T(8,128)} fusion(f32[2048,256]{1,0:T(8,128)} %all-gather.2.cloned.1.call-done, s32[2048]{0:T(1024)S(1)} %broadcast_clamp_fusion), kind=kCustom, calls=%fused_computation.1 | custom fusion | bytes 4202496 | tf_op jit(solution)/shard_map/jit(_take)/gather | solution.py:26
  379.5 1.9 broadcast_select_fusion
  381.4 7.3 %gather_fusion.2 = f32[64,256,256]{2,1,0:T(8,128)} fusion(f32[8,256,256]{2,1,0:T(8,128)S(1)} %broadcast_select_fusion, s32[1024]{0:T(1024)S(1)} %pad_clamp_fusion), kind=kCustom, calls=%fused_computation.2 | custom fusion | bytes 33554688 | tf_op jit(solution)/shard_map/jit(_take)/gather | solution.py:29
  388.7 18.4 %fusion = f32[64,256,128]{1,2,0:T(8,128)} fusion(f32[64,128,256]{2,1,0:T(8,128)} %bitcast.17, f32[64,256,256]{2,1,0:T(8,128)} %gather_fusion.2, pred[64]{0:T(512)(128)(4,1)S(1)} %compare_and_fusion.1), kind=kOutput, calls=%fused_computation.3 | convolution fusion | flops 6446645248 | bytes 33554496 | tf_op jit(solution)/shard_map/nrk,nkq->nrq/dot_general | solution.py:31
  407.2 2.7 collective-permute-start
  409.9 180.2 %collective-permute-done = f32[8192,256]{1,0:T(8,128)} collective-permute-done((f32[8192,256]{1,0:T(8,128)}, f32[8192,256]{1,0:T(8,128)}, u32[]{:S(2)}, u32[]{:S(2)}) %collective-permute-start) | collective-permute-done | bytes 8388640 | tf_op jit(solution)/shard_map/ppermute | solution.py:14
  590.1 67.3 %rev.3 = f32[8192,256]{1,0:T(8,128)} reverse(f32[8192,256]{1,0:T(8,128)} %collective-permute-done), dimensions={1} | reverse | bytes 16777216 | tf_op jit(solution)/shard_map/rev | solution.py:40
  657.4 10.2 %multiply_add_fusion = f32[8192,256]{1,0:T(8,128)} fusion(f32[8192,256]{1,0:T(8,128)} %rev.3, f32[]{:T(128)S(6)} %convert_element_type.3, f32[64,256,128]{1,2,0:T(8,128)} %fusion), kind=kLoop, calls=%fused_computation.5 | loop fusion | flops 4194304 | bytes 25165828 | tf_op jit(solution)/shard_map/add | solution.py:40
  (11 shorter events, 0.1 us)
Async XLA Ops:
  6.5 2.8 copy-start
  6.5 14.6 %copy-start.1 = (s32[64]{0:T(128)S(1)}, s32[64]{0:T(128)}, u32[]{:S(2)}) copy-start(s32[64]{0:T(128)} %param.7) | copy-start | bytes 772
  6.5 362.7 %all-gather.2.cloned.1.call-start = ((), (), s32[]{:S(2)}) async-start(), calls=%async_computation | async-start | bytes 2113536 | tf_op jit(solution)/shard_map/all_gather | solution.py:21
  407.2 182.9 %collective-permute-start = (f32[8192,256]{1,0:T(8,128)}, f32[8192,256]{1,0:T(8,128)}, u32[]{:S(2)}, u32[]{:S(2)}) collective-permute-start(f32[8192,256]{1,0:T(8,128)} %bitcast.7), channel_id=1, source_target_pairs={{0,1},{1,0},{2,3},{3,2},{4,5},{5,4},{6,7},{7,6},{8,9},{9,8},{10,11... | collective-permute-start | bytes 25165832 | tf_op jit(solution)/shard_map/ppermute | solution.py:14
Sparse Core Ops, SparseCore 0:
  9.2 360.0 all-gather.1
where the time goes:
time: 683 us; the launch traced here: 674 us
  waiting for transfers between devices  529 us (77%)
  local copies, waits for them, and re-layouts  96.7 us (14%)
  matrix products  18.4 us (3%)
  other arithmetic  14.2 us (2%)
  between operations  13.5 us (2%)
    all_gather x1, waiting for transfers between devices, on_device(): gathered = lax.all_gather(amplitudes, ('aa', 'ba'), axis=0, tiled=True)  348 us
    ppermute x1, waiting for transfers between devices, partner(): return lax.ppermute(block, axis, route)  180 us
    rev x1, local copies, waits for them, and re-layouts, on_device(): result = partner_result[:, ::-1] + parity * result  67.3 us
    dot_general x1, matrix products, on_device(): jnp.einsum('nrk,nkq->nrq', slab_blocks, per_block, precision=lax.Precisio...  18.4 us
  transfers between devices with their start and end apart: 2, of which 2 were waited for; matrix products, arithmetic and copies ran while one was open for 2% of the time, Pallas kernels for 0%

commit v1 on v0

v1 whole, which is shorter than its diff:
```python
import functools

import jax
import jax.numpy as jnp
import numpy as np
from jax import lax
from jax.experimental import pallas as pl
from jax.experimental.pallas import tpu as pltpu
from jax.sharding import PartitionSpec as P

CORE = 8
Z1, Z2, Z7, X1, Y1, Y3 = 1, 2, 7, 16, 32, 96
ROUNDS = ((Z7, Y3), (Z2, Z1), (X1, Y1))

CHUNK = 512


def trade(block, mask):
    return lax.ppermute(block, ("aa", "ba"), [(i, i ^ mask) for i in range(128)])


def slot_bits():
    masks = [m for pair in ROUNDS for m in pair] + [CORE]
    source_of = np.zeros(128, np.int64)
    for slot in range(128):
        for bit, mask in enumerate(masks):
            if slot >> bit & 1:
                source_of[slot] ^= mask
    slot_of = np.argsort(source_of)
    return [int(slot_of[1 << bit]) for bit in range(7)]


def ladder_kernel(slots, cd_irrep, row_irrep, integrals, gathered, out, block_of, a_buf, picked, high, low, o_buf, a_sem, o_sem):
    count = integrals.shape[0] // CHUNK
    block = picked.shape[1] // 16

    def fetch(i):
        at = pl.ds(i * CHUNK, CHUNK)
        return pltpu.make_async_copy(integrals.at[at], a_buf.at[at], a_sem.at[i])

    def flush(i):
        at = pl.ds(i * CHUNK, CHUNK)
        return pltpu.make_async_copy(o_buf.at[at], out.at[at], o_sem.at[i])

    for i in range(count):
        fetch(i).start()

    for s in range(16):
        block_of[s] = -1
    for b in range(16):
        s = cd_irrep[b]
        half = jnp.where(block_of[2 * s] < 0, 0, 1)
        block_of[2 * s + half] = b

    def pick(q, carry):
        base = block_of[q] * block

        def rows(t, carry):
            for k in range(16):
                j = t * 16 + k
                r = slots[base + j]
                picked[0, pl.ds(q * block + j, 1), :] = gathered[pl.ds(r, 1), :]
                picked[1, pl.ds(q * block + j, 1), :] = gathered[pl.ds(r + 16, 1), :]
            return carry

        return lax.fori_loop(0, block // 16, rows, carry)

    lax.fori_loop(0, 16, pick, 0)

    def split(s, carry):
        for c in range(2):
            v = picked[c, pl.ds(s * 2 * block, 2 * block), :]
            hi = v.astype(jnp.bfloat16)
            high[s, :, c * 128 : c * 128 + 128] = hi
            low[s, :, c * 128 : c * 128 + 128] = (v - hi.astype(jnp.float32)).astype(jnp.bfloat16)
        return carry

    lax.fori_loop(0, 8, split, 0)
    dot = functools.partial(jnp.dot, preferred_element_type=jnp.float32)

    def step(i, carry):
        fetch(i).wait()
        for k in range(CHUNK // block):
            at = pl.ds(pl.multiple_of(i * CHUNK + k * block, block), block)
            a = a_buf[at, :]
            a_hi = a.astype(jnp.bfloat16)
            a_lo = (a - a_hi.astype(jnp.float32)).astype(jnp.bfloat16)
            s = row_irrep[i * (CHUNK // block) + k]
            o_buf[at, :] = dot(a_hi, low[s]) + dot(a_lo, high[s]) + dot(a_hi, high[s])
        flush(i).start()
        return carry

    lax.fori_loop(0, count, step, 0)
    for i in range(count):
        flush(i).wait()


def ladder(slots, cd_irrep, row_irrep, integrals, gathered):
    rows = integrals.shape[0]
    smem = pl.BlockSpec(memory_space=pltpu.SMEM)
    hbm = pl.BlockSpec(memory_space=pl.ANY)
    return pl.pallas_call(
        ladder_kernel,
        out_shape=jax.ShapeDtypeStruct((rows, 256), jnp.float32),
        in_specs=[smem, smem, smem, hbm, pl.BlockSpec(memory_space=pltpu.VMEM)],
        out_specs=hbm,
        scratch_shapes=[
            pltpu.SMEM((16,), jnp.int32),
            pltpu.VMEM((rows, 256), jnp.float32),
            pltpu.VMEM((2, 2048, 128), jnp.float32),
            pltpu.VMEM((8, 256, 256), jnp.bfloat16),
            pltpu.VMEM((8, 256, 256), jnp.bfloat16),
            pltpu.VMEM((rows, 256), jnp.float32),
            pltpu.SemaphoreType.DMA((rows // CHUNK,)),
            pltpu.SemaphoreType.DMA((rows // CHUNK,)),
        ],
        compiler_params=pltpu.CompilerParams(vmem_limit_bytes=40 << 20),
    )(slots, cd_irrep, row_irrep, integrals, gathered)


def on_device(integrals, amplitudes, row_irrep, cd_irrep, cd_order):
    me = lax.axis_index(("aa", "ba"))
    relative = (cd_order >> 4) ^ me
    slot = jnp.zeros_like(cd_order)
    for bit, image in enumerate(slot_bits()):
        slot = slot ^ jnp.where(relative >> bit & 1 == 1, image, 0)
    slots = slot * 32 + (cd_order & 15)

    parity = (1 - 2 * lax.axis_index("ao")).astype(jnp.float32)
    partner = lax.ppermute(amplitudes, "ao", [(0, 1), (1, 0)])
    block = partner[:, ::-1] + parity * amplitudes
    block = jnp.concatenate([block[:, :128], block[:, 128:]])
    for a, b in ROUNDS:
        both = trade(block, a ^ b)
        block = jnp.concatenate([block, trade(block, a), trade(block, b), both])
    block = jnp.concatenate([block, trade(block, CORE)])
    return ladder(slots, cd_irrep, row_irrep, integrals, block)


def solution(mesh):
    placed = (P(("aa", "ba"), None), P(("aa", "ba"), "ao"), P(("aa", "ba")), P(), P())
    return jax.shard_map(
        on_device, mesh=mesh, in_specs=placed, out_specs=P(("aa", "ba"), "ao"), check_vma=False
    )
```

time: 683 us -> 67.5 us (0.10); the launches traced: 674 us -> 67.4 us
  waiting for transfers between devices: 529 us -> 17.8 us
  local copies, waits for them, and re-layouts: 96.7 us -> 10.8 us
  starting transfers between devices: 2.7 us -> 25.8 us
  matrix products: 18.4 us -> 0 us
  other arithmetic: 14.2 us -> 0.75 us
  between operations: 13.5 us -> 0.05 us
  Pallas kernels: 0 us -> 12.2 us
    all_gather x1 -> x0, waiting for transfers between devices: 348 us -> none  [on_device(): gathered = lax.all_gather(amplitudes, ('aa', 'ba'), axis=0, tiled=True)]
    ppermute x1 -> x11, waiting for transfers between devices: 180 us -> 17.8 us  [the longest x10 16.5 us: trade(): lax.ppermute(block, ('aa', 'ba'), [(i, i ^ mask) for i in range(128)])]
    rev x1, local copies, waits for them, and re-layouts: 67.3 us -> 0.15 us  [on_device(): block = partner[:, ::-1] + parity * amplitudes]
    gather x4 -> x0, local copies, waits for them, and re-layouts: 29.3 us -> none  [the longest x2 11.8 us: on_device(): amp_rows = jnp.take(cd_order, columns)]
    ppermute x1 -> x11, starting transfers between devices: 2.7 us -> 25.8 us  [the longest x10 22.3 us: trade(): lax.ppermute(block, ('aa', 'ba'), [(i, i ^ mask) for i in range(128)])]
    dot_general x1 -> x0, matrix products: 18.4 us -> none  [on_device(): jnp.einsum('nrk,nkq->nrq', slab_blocks, per_block, precision=lax.Precisio...]
    pallas_call x0 -> x1, Pallas kernels: none -> 12.2 us  [ladder(): pl.pallas_call(ladder_kernel, out_shape=jax.ShapeDtypeStruct((rows, 256),...]
    unnamed x4 -> x19, local copies, waits for them, and re-layouts: 0.01 us -> 9.83 us
  transfers between devices with their start and end apart: 2 -> 11, of which waited for: 2 -> 6; matrix products, arithmetic and copies ran while one was open for 2% -> 6% of each run, Pallas kernels for 0% -> 0%
where the time goes in v1:
time: 67.5 us; the launch traced here: 67.4 us
  starting transfers between devices  25.8 us (38%)
  waiting for transfers between devices  17.8 us (26%)
  Pallas kernels  12.2 us (18%)
  local copies, waits for them, and re-layouts  10.8 us (16%)
  other arithmetic  0.75 us (1%)
    ppermute x10, starting transfers between devices, trade(): lax.ppermute(block, ('aa', 'ba'), [(i, i ^ mask) for i in range(128)])  22.3 us
    ppermute x10, waiting for transfers between devices, trade(): lax.ppermute(block, ('aa', 'ba'), [(i, i ^ mask) for i in range(128)])  16.5 us
    pallas_call x1, Pallas kernels, ladder(): pl.pallas_call(ladder_kernel, out_shape=jax.ShapeDtypeStruct((rows, 256),...  12.2 us
    unnamed x19, local copies, waits for them, and re-layouts  9.83 us
    ppermute x1, starting transfers between devices, on_device(): partner = lax.ppermute(amplitudes, 'ao', [(0, 1), (1, 0)])  3.57 us
  transfers between devices with their start and end apart: 11, of which 6 were waited for; matrix products, arithmetic and copies ran while one was open for 6% of the time, Pallas kernels for 0%

profile of v1, /device:TPU:1, one launch (start us, length us, event | category | flops | bytes accessed | tf_op | source)
XLA Modules:
  0.0 67.4 jit_solution(7409114833908192338)
XLA Ops:
  0.0 0.0 copy-start.3
  0.0 3.6 %collective-permute-start = (f32[16,256]{1,0:T(8,128)}, f32[16,256]{1,0:T(8,128)S(1)}, u32[]{:S(2)}, u32[]{:S(2)}) collective-permute-start(f32[16,256]{1,0:T(8,128)} %param.6), channel_id=1, source_target_pairs={{0,1},{1,0},{2,3},{3,2},{4,5},{5,4},{6,7},{7,6},{8,9},{9,8},{10,11... | collective-permute-start | bytes 49160 | tf_op jit(solution)/shard_map/ppermute | solution.py:130
  3.6 1.3 %collective-permute-done = f32[16,256]{1,0:T(8,128)S(1)} collective-permute-done((f32[16,256]{1,0:T(8,128)}, f32[16,256]{1,0:T(8,128)S(1)}, u32[]{:S(2)}, u32[]{:S(2)}) %collective-permute-start) | collective-permute-done | bytes 16416 | tf_op jit(solution)/shard_map/ppermute | solution.py:130
  4.9 0.1 rev.3
  5.1 0.7 %multiply_add_fusion = f32[16,256]{1,0:T(8,128)S(1)} fusion(f32[16,256]{1,0:T(8,128)S(1)} %rev.3, f32[16,256]{1,0:T(8,128)} %param.6, f32[]{:T(128)S(6)} %convert_element_type.3), kind=kLoop, calls=%fused_computation.37 | loop fusion | flops 8192 | bytes 49156 | tf_op jit(solution)/shard_map/add | solution.py:131
  5.8 0.6 constant_dynamic-update-slice_fusion.23
  6.4 0.6 constant_dynamic-update-slice_fusion.22
  7.0 8.3 %collective-permute-start.3 = (f32[32,128]{1,0:T(8,128)S(1)}, f32[32,128]{1,0:T(8,128)S(1)}, u32[]{:S(2)}, u32[]{:S(2)}) collective-permute-start(f32[32,128]{1,0:T(8,128)S(1)} %pad_maximum_fusion), channel_id=1, source_target_pairs={{0,206},{2,204},{4,202},{6,200},{8,198},{10,196},{12,194},{14,192}... | collective-permute-start | bytes 49160 | tf_op jit(solution)/shard_map/ppermute | solution.py:19
  15.2 0.0 collective-permute-start.2
  15.2 0.3 collective-permute-start.1
  15.5 3.5 %collective-permute-done.1 = f32[32,128]{1,0:T(8,128)S(1)} collective-permute-done((f32[32,128]{1,0:T(8,128)S(1)}, f32[32,128]{1,0:T(8,128)S(1)}, u32[]{:S(2)}, u32[]{:S(2)}) %collective-permute-start.1) | collective-permute-done | bytes 16416 | tf_op jit(solution)/shard_map/ppermute | solution.py:19
  19.0 0.6 constant_dynamic-update-slice_fusion.21
  19.7 0.0 collective-permute-done.2
  19.7 0.6 constant_dynamic-update-slice_fusion.20
  20.3 0.0 collective-permute-done.3
  20.3 0.6 constant_dynamic-update-slice_fusion.19
  20.9 3.9 %collective-permute-start.4 = (f32[128,128]{1,0:T(8,128)S(1)}, f32[128,128]{1,0:T(8,128)S(1)}, u32[]{:S(2)}, u32[]{:S(2)}) collective-permute-start(f32[128,128]{1,0:T(8,128)S(1)} %get-tuple-element.23), channel_id=1, source_target_pairs={{0,4},{2,6},{4,0},{6,2},{8,12},{10,14},{12,8},{14,10},{16,20},{18,... | collective-permute-start | bytes 196616 | tf_op jit(solution)/shard_map/ppermute | solution.py:19
  24.8 1.6 %collective-permute-start.6 = (f32[128,128]{1,0:T(8,128)S(1)}, f32[128,128]{1,0:T(8,128)S(1)}, u32[]{:S(2)}, u32[]{:S(2)}) collective-permute-start(f32[128,128]{1,0:T(8,128)S(1)} %get-tuple-element.23), channel_id=1, source_target_pairs={{0,6},{2,4},{4,2},{6,0},{8,14},{10,12},{12,10},{14,8},{16,22},{18,... | collective-permute-start | bytes 196616 | tf_op jit(solution)/shard_map/ppermute | solution.py:19
  26.4 0.0 collective-permute-start.5
  26.4 0.0 collective-permute-done.4
  26.4 0.6 constant_dynamic-update-slice_fusion.18
  27.1 3.9 %collective-permute-done.5 = f32[128,128]{1,0:T(8,128)S(1)} collective-permute-done((f32[128,128]{1,0:T(8,128)S(1)}, f32[128,128]{1,0:T(8,128)S(1)}, u32[]{:S(2)}, u32[]{:S(2)}) %collective-permute-start.5) | collective-permute-done | bytes 65568 | tf_op jit(solution)/shard_map/ppermute | solution.py:19
  30.9 0.6 constant_dynamic-update-slice_fusion.17
  31.6 0.0 collective-permute-done.6
  31.6 0.6 constant_dynamic-update-slice_fusion.16
  32.2 1.2 %collective-permute-start.7 = (f32[512,128]{1,0:T(8,128)S(1)}, f32[512,128]{1,0:T(8,128)S(1)}, u32[]{:S(2)}, u32[]{:S(2)}) collective-permute-start(f32[512,128]{1,0:T(8,128)S(1)} %get-tuple-element.13), channel_id=1, source_target_pairs={{0,32},{2,34},{4,36},{6,38},{8,40},{10,42},{12,44},{14,46},{16,48}... | collective-permute-start | bytes 786440 | tf_op jit(solution)/shard_map/ppermute | solution.py:19
  33.4 0.0 collective-permute-start.8
  33.4 1.4 %collective-permute-start.9 = (f32[512,128]{1,0:T(8,128)S(1)}, f32[512,128]{1,0:T(8,128)S(1)}, u32[]{:S(2)}, u32[]{:S(2)}) collective-permute-start(f32[512,128]{1,0:T(8,128)S(1)} %get-tuple-element.13), channel_id=1, source_target_pairs={{0,96},{2,98},{4,100},{6,102},{8,104},{10,106},{12,108},{14,110},{... | collective-permute-start | bytes 786440 | tf_op jit(solution)/shard_map/ppermute | solution.py:19
  34.9 2.6 %collective-permute-done.7 = f32[512,128]{1,0:T(8,128)S(1)} collective-permute-done((f32[512,128]{1,0:T(8,128)S(1)}, f32[512,128]{1,0:T(8,128)S(1)}, u32[]{:S(2)}, u32[]{:S(2)}) %collective-permute-start.7) | collective-permute-done | bytes 262176 | tf_op jit(solution)/shard_map/ppermute | solution.py:19
  37.4 0.0 copy-start.1
  37.4 0.0 copy-start.2
  37.4 0.7 %constant_dynamic-update-slice_fusion.15 = (f32[2048,128]{1,0:T(8,128)}, f32[4096,128]{1,0:T(8,128)S(1)}) fusion(f32[2048,128]{1,0:T(8,128)} %get-tuple-element.11, f32[512,128]{1,0:T(8,128)S(1)} %collective-permute-done.7, f32[4096,128]{1,0:T(8,128)S(1)} %get-tuple-element.12), kind=kLoop, calls=%fused_computation.15 | loop fusion | bytes 786432
  38.2 4.0 %collective-permute-done.8 = f32[512,128]{1,0:T(8,128)S(1)} collective-permute-done((f32[512,128]{1,0:T(8,128)S(1)}, f32[512,128]{1,0:T(8,128)S(1)}, u32[]{:S(2)}, u32[]{:S(2)}) %collective-permute-start.8) | collective-permute-done | bytes 262176 | tf_op jit(solution)/shard_map/ppermute | solution.py:19
  42.2 0.7 %constant_dynamic-update-slice_fusion.14 = (f32[2048,128]{1,0:T(8,128)}, f32[4096,128]{1,0:T(8,128)S(1)}) fusion(f32[2048,128]{1,0:T(8,128)} %get-tuple-element.9, f32[512,128]{1,0:T(8,128)S(1)} %collective-permute-done.8, f32[4096,128]{1,0:T(8,128)S(1)} %get-tuple-element.10), kind=kLoop, calls=%fused_computation.14 | loop fusion | bytes 786432
  42.9 0.0 collective-permute-done.9
  42.9 0.7 %constant_dynamic-update-slice_fusion.13 = (f32[2048,128]{1,0:T(8,128)}, f32[4096,128]{1,0:T(8,128)S(1)}) fusion(f32[2048,128]{1,0:T(8,128)} %get-tuple-element.7, f32[512,128]{1,0:T(8,128)S(1)} %collective-permute-done.9, f32[4096,128]{1,0:T(8,128)S(1)} %get-tuple-element.8), kind=kLoop, calls=%fused_computation.13 | loop fusion | bytes 786432 | tf_op jit(solution)/shard_map/concatenate | solution.py:135
  43.7 5.6 %collective-permute-start.10 = (f32[2048,128]{1,0:T(8,128)}, f32[2048,128]{1,0:T(8,128)S(1)}, u32[]{:S(2)}, u32[]{:S(2)}) collective-permute-start(f32[2048,128]{1,0:T(8,128)} %get-tuple-element.5), channel_id=1, source_target_pairs={{0,16},{2,18},{4,20},{6,22},{8,24},{10,26},{12,28},{14,30},{16,0},... | collective-permute-start | bytes 3145736 | tf_op jit(solution)/shard_map/ppermute | solution.py:19
  49.2 0.0 copy-done.3
  49.3 2.5 %collective-permute-done.10 = f32[2048,128]{1,0:T(8,128)S(1)} collective-permute-done((f32[2048,128]{1,0:T(8,128)}, f32[2048,128]{1,0:T(8,128)S(1)}, u32[]{:S(2)}, u32[]{:S(2)}) %collective-permute-start.10) | collective-permute-done | bytes 1048608 | tf_op jit(solution)/shard_map/ppermute | solution.py:19
  51.7 0.1 constant_dynamic-update-slice_fusion.24.gathered
  51.8 0.0 copy-done.1
  51.8 0.0 copy-done.2
  51.8 0.0 copy-start
  51.8 3.4 %copy-done = f32[8192,256]{1,0:T(8,128)S(1)} copy-done((f32[8192,256]{1,0:T(8,128)S(1)}, f32[8192,256]{1,0:T(8,128)}, u32[]{:S(2)}) %copy-start) | copy-done | bytes 8388632
  55.2 12.2 %shard_map.55 = f32[8192,256]{1,0:T(8,128)} custom-call(s32[2048]{0:T(1024)S(1)} %and_add_fusion.slots, s32[16]{0:T(128)S(1)} %copy-done.1, s32[64]{0:T(128)S(1)} %copy-done.2, f32[8192,256]{1,0:T(8,128)S(1)} %copy-done, f32[4096,128]{1,0:T(8,128)S(1)} %constant_dynamic-update-slice_fusion.24.gathered), custom_call_target="tpu_custom_call" | custom-call | tf_op jit(solution)/shard_map/pallas_call | solution.py:102
  (3 shorter events, 0.0 us)
Async XLA Ops:
  0.0 49.2 %copy-start.3 = (s32[2048]{0:T(1024)S(1)}, s32[2048]{0:T(1024)}, u32[]{:S(2)}) copy-start(s32[2048]{0:T(1024)} %param.9) | copy-start | bytes 24580
  0.0 4.9 %collective-permute-start = (f32[16,256]{1,0:T(8,128)}, f32[16,256]{1,0:T(8,128)S(1)}, u32[]{:S(2)}, u32[]{:S(2)}) collective-permute-start(f32[16,256]{1,0:T(8,128)} %param.6), channel_id=1, source_target_pairs={{0,1},{1,0},{2,3},{3,2},{4,5},{5,4},{6,7},{7,6},{8,9},{9,8},{10,11... | collective-permute-start | bytes 49160 | tf_op jit(solution)/shard_map/ppermute | solution.py:130
  7.0 13.3 %collective-permute-start.3 = (f32[32,128]{1,0:T(8,128)S(1)}, f32[32,128]{1,0:T(8,128)S(1)}, u32[]{:S(2)}, u32[]{:S(2)}) collective-permute-start(f32[32,128]{1,0:T(8,128)S(1)} %pad_maximum_fusion), channel_id=1, source_target_pairs={{0,206},{2,204},{4,202},{6,200},{8,198},{10,196},{12,194},{14,192}... | collective-permute-start | bytes 49160 | tf_op jit(solution)/shard_map/ppermute | solution.py:19
  15.2 4.4 %collective-permute-start.2 = (f32[32,128]{1,0:T(8,128)S(1)}, f32[32,128]{1,0:T(8,128)S(1)}, u32[]{:S(2)}, u32[]{:S(2)}) collective-permute-start(f32[32,128]{1,0:T(8,128)S(1)} %pad_maximum_fusion), channel_id=1, source_target_pairs={{0,192},{2,194},{4,196},{6,198},{8,200},{10,202},{12,204},{14,206}... | collective-permute-start | bytes 49160 | tf_op jit(solution)/shard_map/ppermute | solution.py:19
  15.2 3.8 %collective-permute-start.1 = (f32[32,128]{1,0:T(8,128)S(1)}, f32[32,128]{1,0:T(8,128)S(1)}, u32[]{:S(2)}, u32[]{:S(2)}) collective-permute-start(f32[32,128]{1,0:T(8,128)S(1)} %pad_maximum_fusion), channel_id=1, source_target_pairs={{0,14},{2,12},{4,10},{6,8},{8,6},{10,4},{12,2},{14,0},{16,30},{18,... | collective-permute-start | bytes 49160 | tf_op jit(solution)/shard_map/ppermute | solution.py:19
  20.9 5.5 %collective-permute-start.4 = (f32[128,128]{1,0:T(8,128)S(1)}, f32[128,128]{1,0:T(8,128)S(1)}, u32[]{:S(2)}, u32[]{:S(2)}) collective-permute-start(f32[128,128]{1,0:T(8,128)S(1)} %get-tuple-element.23), channel_id=1, source_target_pairs={{0,4},{2,6},{4,0},{6,2},{8,12},{10,14},{12,8},{14,10},{16,20},{18,... | collective-permute-start | bytes 196616 | tf_op jit(solution)/shard_map/ppermute | solution.py:19
  24.8 6.8 %collective-permute-start.6 = (f32[128,128]{1,0:T(8,128)S(1)}, f32[128,128]{1,0:T(8,128)S(1)}, u32[]{:S(2)}, u32[]{:S(2)}) collective-permute-start(f32[128,128]{1,0:T(8,128)S(1)} %get-tuple-element.23), channel_id=1, source_target_pairs={{0,6},{2,4},{4,2},{6,0},{8,14},{10,12},{12,10},{14,8},{16,22},{18,... | collective-permute-start | bytes 196616 | tf_op jit(solution)/shard_map/ppermute | solution.py:19
  26.4 4.5 %collective-permute-start.5 = (f32[128,128]{1,0:T(8,128)S(1)}, f32[128,128]{1,0:T(8,128)S(1)}, u32[]{:S(2)}, u32[]{:S(2)}) collective-permute-start(f32[128,128]{1,0:T(8,128)S(1)} %get-tuple-element.23), channel_id=1, source_target_pairs={{0,2},{2,0},{4,6},{6,4},{8,10},{10,8},{12,14},{14,12},{16,18},{18,... | collective-permute-start | bytes 196616 | tf_op jit(solution)/shard_map/ppermute | solution.py:19
  32.2 5.2 %collective-permute-start.7 = (f32[512,128]{1,0:T(8,128)S(1)}, f32[512,128]{1,0:T(8,128)S(1)}, u32[]{:S(2)}, u32[]{:S(2)}) collective-permute-start(f32[512,128]{1,0:T(8,128)S(1)} %get-tuple-element.13), channel_id=1, source_target_pairs={{0,32},{2,34},{4,36},{6,38},{8,40},{10,42},{12,44},{14,46},{16,48}... | collective-permute-start | bytes 786440 | tf_op jit(solution)/shard_map/ppermute | solution.py:19
  33.4 8.8 %collective-permute-start.8 = (f32[512,128]{1,0:T(8,128)S(1)}, f32[512,128]{1,0:T(8,128)S(1)}, u32[]{:S(2)}, u32[]{:S(2)}) collective-permute-start(f32[512,128]{1,0:T(8,128)S(1)} %get-tuple-element.13), channel_id=1, source_target_pairs={{0,64},{2,66},{4,68},{6,70},{8,72},{10,74},{12,76},{14,78},{16,80}... | collective-permute-start | bytes 786440 | tf_op jit(solution)/shard_map/ppermute | solution.py:19
  33.4 9.5 %collective-permute-start.9 = (f32[512,128]{1,0:T(8,128)S(1)}, f32[512,128]{1,0:T(8,128)S(1)}, u32[]{:S(2)}, u32[]{:S(2)}) collective-permute-start(f32[512,128]{1,0:T(8,128)S(1)} %get-tuple-element.13), channel_id=1, source_target_pairs={{0,96},{2,98},{4,100},{6,102},{8,104},{10,106},{12,108},{14,110},{... | collective-permute-start | bytes 786440 | tf_op jit(solution)/shard_map/ppermute | solution.py:19
  37.4 14.4 %copy-start.1 = (s32[16]{0:T(128)S(1)}, s32[16]{0:T(128)}, u32[]{:S(2)}) copy-start(s32[16]{0:T(128)} %cd_irrep.1) | copy-start | bytes 196
  37.4 14.4 %copy-start.2 = (s32[64]{0:T(128)S(1)}, s32[64]{0:T(128)}, u32[]{:S(2)}) copy-start(s32[64]{0:T(128)} %row_irrep.1) | copy-start | bytes 772
  43.7 8.1 %collective-permute-start.10 = (f32[2048,128]{1,0:T(8,128)}, f32[2048,128]{1,0:T(8,128)S(1)}, u32[]{:S(2)}, u32[]{:S(2)}) collective-permute-start(f32[2048,128]{1,0:T(8,128)} %get-tuple-element.5), channel_id=1, source_target_pairs={{0,16},{2,18},{4,20},{6,22},{8,24},{10,26},{12,28},{14,30},{16,0},... | collective-permute-start | bytes 3145736 | tf_op jit(solution)/shard_map/ppermute | solution.py:19
  51.8 3.4 %copy-start = (f32[8192,256]{1,0:T(8,128)S(1)}, f32[8192,256]{1,0:T(8,128)}, u32[]{:S(2)}) copy-start(f32[8192,256]{1,0:T(8,128)} %integrals.1) | copy-start | bytes 25165828

commit v2 on v1

v2 whole, which is shorter than its diff:
```python
import functools

import jax
import jax.numpy as jnp
import numpy as np
from jax import lax
from jax.experimental import pallas as pl
from jax.experimental.pallas import tpu as pltpu
from jax.sharding import PartitionSpec as P

CORE = 8
Z1, Z2, Z7, X1, Y1, Y3 = 1, 2, 7, 16, 32, 96
STEPS = ((Z7, Z7), (Z2, Z2), (Y3, X1), (Z1, Y1), (X1, Z1), (Y1, Y3))

CHUNK = 512
STRIDE = 2048


def trade(block, masks):
    return lax.ppermute(block, ("aa", "ba"), [(i, i ^ masks[i // CORE % 2]) for i in range(128)])


def slot_bits(core):
    masks = [step[core] for step in STEPS]
    source_of = {}
    for slot in range(64):
        source = 0
        for bit, mask in enumerate(masks):
            if slot >> bit & 1:
                source ^= mask
        source_of[source] = slot
    return [0 if 1 << bit == CORE else source_of[1 << bit] for bit in range(7)]


def ladder_kernel(slots, cd_irrep, row_irrep, a_hi, a_lo, *rest):
    pieces, (out, block_of, gathered, picked, high, low, o_buf, o_sem) = rest[:8], rest[8:]
    rows = out.shape[0]
    block = picked.shape[1] // 16
    size = pieces[0].shape[0]

    def flush(i):
        at = pl.ds(i * CHUNK, CHUNK)
        return pltpu.make_async_copy(o_buf.at[at], out.at[at], o_sem.at[i])

    for i, piece in enumerate(pieces):
        gathered[i * size : (i + 1) * size, :] = piece[...]
    for s in range(16):
        block_of[s] = -1
    for b in range(16):
        s = cd_irrep[b]
        half = jnp.where(block_of[2 * s] < 0, 0, 1)
        block_of[2 * s + half] = b

    def pick(q, carry):
        base = block_of[q] * block

        def some(t, carry):
            for k in range(16):
                j = t * 16 + k
                r = slots[base + j]
                picked[0, pl.ds(q * block + j, 1), :] = gathered[pl.ds(r, 1), :]
                picked[1, pl.ds(q * block + j, 1), :] = gathered[pl.ds(r + 16, 1), :]
            return carry

        return lax.fori_loop(0, block // 16, some, carry)

    lax.fori_loop(0, 16, pick, 0)

    def split(s, carry):
        for c in range(2):
            v = picked[c, pl.ds(s * 2 * block, 2 * block), :]
            hi = v.astype(jnp.bfloat16)
            high[s, :, c * 128 : c * 128 + 128] = hi
            low[s, :, c * 128 : c * 128 + 128] = (v - hi.astype(jnp.float32)).astype(jnp.bfloat16)
        return carry

    lax.fori_loop(0, 8, split, 0)

    def step(i, carry):
        for k in range(STRIDE // block):
            at = pl.ds(pl.multiple_of(i * STRIDE + k * block, block), block)
            s = row_irrep[i * (STRIDE // block) + k]
            hi, b_hi = a_hi[at, :], high[s]
            left = jnp.concatenate([hi, a_lo[at, :], hi], axis=1)
            right = jnp.concatenate([low[s], b_hi, b_hi], axis=0)
            o_buf[at, :] = jnp.dot(left, right, preferred_element_type=jnp.float32)
            done = (k + 1) * block - CHUNK
            if done > 0 and done % CHUNK == 0:
                flush(i * (STRIDE // CHUNK) + done // CHUNK - 1).start()
        flush((i + 1) * (STRIDE // CHUNK) - 1).start()
        return carry

    lax.fori_loop(0, rows // STRIDE, step, 0)
    for i in range(rows // CHUNK):
        flush(i).wait()


def ladder(slots, cd_irrep, row_irrep, a_hi, a_lo, pieces):
    rows = a_hi.shape[0]
    smem = pl.BlockSpec(memory_space=pltpu.SMEM)
    vmem = pl.BlockSpec(memory_space=pltpu.VMEM)
    return pl.pallas_call(
        ladder_kernel,
        out_shape=jax.ShapeDtypeStruct((rows, 256), jnp.float32),
        in_specs=[smem] * 3 + [vmem] * (2 + len(pieces)),
        out_specs=pl.BlockSpec(memory_space=pl.ANY),
        scratch_shapes=[
            pltpu.SMEM((16,), jnp.int32),
            pltpu.VMEM((4096, 128), jnp.float32),
            pltpu.VMEM((2, 2048, 128), jnp.float32),
            pltpu.VMEM((8, 256, 256), jnp.bfloat16),
            pltpu.VMEM((8, 256, 256), jnp.bfloat16),
            pltpu.VMEM((rows, 256), jnp.float32),
            pltpu.SemaphoreType.DMA((rows // CHUNK,)),
        ],
        compiler_params=pltpu.CompilerParams(vmem_limit_bytes=32 << 20),
    )(slots, cd_irrep, row_irrep, a_hi, a_lo, *pieces)


def on_device(integrals, amplitudes, row_irrep, cd_irrep, cd_order):
    rounded = lax.reduce_precision(integrals, exponent_bits=8, mantissa_bits=7)
    a_hi = rounded.astype(jnp.bfloat16)
    a_lo = (integrals - rounded).astype(jnp.bfloat16)

    me = lax.axis_index(("aa", "ba"))
    source = cd_order >> 4
    relative = source ^ me
    source_core = source >> 3 & 1
    slot = (relative >> 3 & 1) << 6
    for bit, (zero, one) in enumerate(zip(slot_bits(0), slot_bits(1))):
        image = jnp.where(source_core == 1, one, zero)
        slot = slot ^ jnp.where(relative >> bit & 1 == 1, image, 0)
    slots = slot * 32 + (cd_order & 15)

    parity = (1 - 2 * lax.axis_index("ao")).astype(jnp.float32)
    partner = lax.ppermute(amplitudes, "ao", [(0, 1), (1, 0)])
    partner, a_hi, a_lo = lax.optimization_barrier((partner, a_hi, a_lo))
    block = partner[:, ::-1] + parity * amplitudes
    block = jnp.concatenate([block[:, :128], block[:, 128:]])
    for masks in STEPS[:-2]:
        block = lax.optimization_barrier(jnp.concatenate([block, trade(block, masks)]))
    a, b = STEPS[-2:]
    both = tuple(p ^ q for p, q in zip(a, b))
    pieces = [block, trade(block, a), trade(block, b), trade(block, both)]
    pieces += [trade(piece, (CORE, CORE)) for piece in pieces]
    return ladder(slots, cd_irrep, row_irrep, a_hi, a_lo, pieces)


def solution(mesh):
    placed = (P(("aa", "ba"), None), P(("aa", "ba"), "ao"), P(("aa", "ba")), P(), P())
    return jax.shard_map(
        on_device, mesh=mesh, in_specs=placed, out_specs=P(("aa", "ba"), "ao"), check_vma=False
    )
```

time: 67.5 us -> 62.4 us (0.924)
  waiting for transfers between devices: 17.8 us -> 9.54 us
  other arithmetic: 0.75 us -> 8.13 us
  local copies, waits for them, and re-layouts: 10.8 us -> 4.55 us
  starting transfers between devices: 25.8 us -> 30.4 us
  Pallas kernels: 12.2 us -> 9.52 us
    convert_element_type x0 -> x1, other arithmetic: none -> 8.07 us  [on_device(): a_lo = (integrals - rounded).astype(jnp.bfloat16)]
    ppermute x10 -> x11, waiting for transfers between devices: 16.5 us -> 9.54 us  [trade(): lax.ppermute(block, ('aa', 'ba'), [(i, i ^ masks[i // CORE % 2]) for i in...]
    unnamed x19 -> x12, local copies, waits for them, and re-layouts: 9.83 us -> 4.39 us
    ppermute x10 -> x11, starting transfers between devices: 22.3 us -> 26.7 us  [trade(): lax.ppermute(block, ('aa', 'ba'), [(i, i ^ masks[i // CORE % 2]) for i in...]
    pallas_call x1, Pallas kernels: 12.2 us -> 9.52 us  [ladder(): pl.pallas_call(ladder_kernel, out_shape=jax.ShapeDtypeStruct((rows, 256),...]
    ppermute x1, waiting for transfers between devices: 1.34 us -> 0.01 us  [on_device(): partner = lax.ppermute(amplitudes, 'ao', [(0, 1), (1, 0)])]
    concatenate x2 -> x0, local copies, waits for them, and re-layouts: 0.81 us -> none  [the longest x1 0.74 us: on_device(): block = jnp.concatenate([block, trade(block, a), trade(block, b), both])]
    add x1, other arithmetic: 0.73 us -> 0.01 us  [on_device(): block = partner[:, ::-1] + parity * amplitudes]
  transfers between devices with their start and end apart: 11 -> 12, of which waited for: 6 -> 6; matrix products, arithmetic and copies ran while one was open for 6% -> 13% of each run, Pallas kernels for 0% -> 0%
where the time goes in v2:
time: 62.4 us; the launch traced here: 62.2 us
  starting transfers between devices  30.4 us (49%)
  waiting for transfers between devices  9.54 us (15%)
  Pallas kernels  9.52 us (15%)
  other arithmetic  8.13 us (13%)
  local copies, waits for them, and re-layouts  4.55 us (7%)
    ppermute x11, starting transfers between devices, trade(): lax.ppermute(block, ('aa', 'ba'), [(i, i ^ masks[i // CORE % 2]) for i in...  26.7 us
    ppermute x11, waiting for transfers between devices, trade(): lax.ppermute(block, ('aa', 'ba'), [(i, i ^ masks[i // CORE % 2]) for i in...  9.54 us
    pallas_call x1, Pallas kernels, ladder(): pl.pallas_call(ladder_kernel, out_shape=jax.ShapeDtypeStruct((rows, 256),...  9.52 us
    convert_element_type x1, other arithmetic, on_device(): a_lo = (integrals - rounded).astype(jnp.bfloat16)  8.07 us
    unnamed x12, local copies, waits for them, and re-layouts  4.39 us
    ppermute x1, starting transfers between devices, on_device(): partner = lax.ppermute(amplitudes, 'ao', [(0, 1), (1, 0)])  3.66 us
  transfers between devices with their start and end apart: 12, of which 6 were waited for; matrix products, arithmetic and copies ran while one was open for 13% of the time, Pallas kernels for 0%

profile of v2, /device:TPU:1, one launch (start us, length us, event | category | flops | bytes accessed | tf_op | source)
XLA Modules:
  0.0 62.2 jit_solution(16998097816514725496)
XLA Ops:
  0.0 0.0 copy-start.4
  0.0 0.0 copy-start.5
  0.0 0.0 copy-start.2
  0.0 0.0 copy-start.3
  0.0 3.7 %collective-permute-start = (f32[16,256]{1,0:T(8,128)}, f32[16,256]{1,0:T(8,128)S(1)}, u32[]{:S(2)}, u32[]{:S(2)}) collective-permute-start(f32[16,256]{1,0:T(8,128)} %param.6), channel_id=1, source_target_pairs={{0,1},{1,0},{2,3},{3,2},{4,5},{5,4},{6,7},{7,6},{8,9},{9,8},{10,11... | collective-permute-start | bytes 49160 | tf_op jit(solution)/shard_map/ppermute | solution.py:136
  3.7 8.1 %fusion = (bf16[8192,256]{1,0:T(8,128)(2,1)}, bf16[8192,256]{1,0:T(8,128)(2,1)}) fusion(f32[8192,256]{1,0:T(8,128)} %param.5), kind=kLoop, calls=%fused_computation.2 | loop fusion | flops 8388608 | bytes 16777216 | tf_op jit(solution)/shard_map/convert_element_type | solution.py:123
  11.7 0.0 collective-permute-done
  11.8 0.2 rev.3
  11.9 0.0 copy-done.4
  11.9 5.7 %collective-permute-start.1 = (f32[32,128]{1,0:T(8,128)S(1)}, f32[32,128]{1,0:T(8,128)S(1)}, u32[]{:S(2)}, u32[]{:S(2)}) collective-permute-start(f32[32,128]{1,0:T(8,128)S(1)} %pad_maximum_fusion.4), channel_id=1, source_target_pairs={{0,14},{2,12},{4,10},{6,8},{8,6},{10,4},{12,2},{14,0},{16,30},{18,... | collective-permute-start | bytes 49160 | tf_op jit(solution)/shard_map/ppermute | solution.py:20
  17.6 1.1 %collective-permute-done.1 = f32[32,128]{1,0:T(8,128)S(1)} collective-permute-done((f32[32,128]{1,0:T(8,128)S(1)}, f32[32,128]{1,0:T(8,128)S(1)}, u32[]{:S(2)}, u32[]{:S(2)}) %collective-permute-start.1) | collective-permute-done | bytes 16416 | tf_op jit(solution)/shard_map/ppermute | solution.py:20
  18.7 2.1 %collective-permute-start.2 = (f32[64,128]{1,0:T(8,128)S(1)}, f32[64,128]{1,0:T(8,128)S(1)}, u32[]{:S(2)}, u32[]{:S(2)}) collective-permute-start(f32[64,128]{1,0:T(8,128)S(1)} %pad_maximum_fusion.3), channel_id=1, source_target_pairs={{0,4},{2,6},{4,0},{6,2},{8,12},{10,14},{12,8},{14,10},{16,20},{18,... | collective-permute-start | bytes 98312 | tf_op jit(solution)/shard_map/ppermute | solution.py:20
  20.8 1.6 %collective-permute-done.2 = f32[64,128]{1,0:T(8,128)S(1)} collective-permute-done((f32[64,128]{1,0:T(8,128)S(1)}, f32[64,128]{1,0:T(8,128)S(1)}, u32[]{:S(2)}, u32[]{:S(2)}) %collective-permute-start.2) | collective-permute-done | bytes 32800 | tf_op jit(solution)/shard_map/ppermute | solution.py:20
  22.4 0.3 collective-permute-start.3
  22.7 2.8 %collective-permute-done.3 = f32[128,128]{1,0:T(8,128)S(1)} collective-permute-done((f32[128,128]{1,0:T(8,128)S(1)}, f32[128,128]{1,0:T(8,128)S(1)}, u32[]{:S(2)}, u32[]{:S(2)}) %collective-permute-start.3) | collective-permute-done | bytes 65568 | tf_op jit(solution)/shard_map/ppermute | solution.py:20
  25.5 1.4 %collective-permute-start.4 = (f32[256,128]{1,0:T(8,128)S(1)}, f32[256,128]{1,0:T(8,128)S(1)}, u32[]{:S(2)}, u32[]{:S(2)}) collective-permute-start(f32[256,128]{1,0:T(8,128)S(1)} %pad_maximum_fusion.1), channel_id=1, source_target_pairs={{0,2},{2,0},{4,6},{6,4},{8,10},{10,8},{12,14},{14,12},{16,80},{18,... | collective-permute-start | bytes 393224 | tf_op jit(solution)/shard_map/ppermute | solution.py:20
  26.9 2.5 %collective-permute-done.4 = f32[256,128]{1,0:T(8,128)S(1)} collective-permute-done((f32[256,128]{1,0:T(8,128)S(1)}, f32[256,128]{1,0:T(8,128)S(1)}, u32[]{:S(2)}, u32[]{:S(2)}) %collective-permute-start.4) | collective-permute-done | bytes 131104 | tf_op jit(solution)/shard_map/ppermute | solution.py:20
  29.5 4.2 %collective-permute-start.7 = (f32[512,128]{1,0:T(8,128)S(1)}, f32[512,128]{1,0:T(8,128)S(1)}, u32[]{:S(2)}, u32[]{:S(2)}) collective-permute-start(f32[512,128]{1,0:T(8,128)S(1)} %pad_maximum_fusion.rest_0_), channel_id=1, source_target_pairs={{0,96},{2,98},{4,100},{6,102},{8,104},{10,106},{12,108},{14,110},{... | collective-permute-start | bytes 786440 | tf_op jit(solution)/shard_map/ppermute | solution.py:20
  33.6 0.0 collective-permute-start.6
  33.6 0.4 collective-permute-start.5
  34.0 6.4 %collective-permute-start.8 = (f32[512,128]{1,0:T(8,128)S(1)}, f32[512,128]{1,0:T(8,128)S(1)}, u32[]{:S(2)}, u32[]{:S(2)}) collective-permute-start(f32[512,128]{1,0:T(8,128)S(1)} %pad_maximum_fusion.rest_0_), channel_id=1, source_target_pairs={{0,16},{2,18},{4,20},{6,22},{8,24},{10,26},{12,28},{14,30},{16,0},... | collective-permute-start | bytes 786440 | tf_op jit(solution)/shard_map/ppermute | solution.py:20
  40.4 0.0 collective-permute-done.7.rest_3_
  40.4 3.9 %collective-permute-start.11 = (f32[512,128]{1,0:T(8,128)S(1)}, f32[512,128]{1,0:T(8,128)S(1)}, u32[]{:S(2)}, u32[]{:S(2)}) collective-permute-start(f32[512,128]{1,0:T(8,128)S(1)} %collective-permute-done.7.rest_3_), channel_id=1, source_target_pairs={{0,16},{2,18},{4,20},{6,22},{8,24},{10,26},{12,28},{14,30},{16,0},... | collective-permute-start | bytes 786440 | tf_op jit(solution)/shard_map/ppermute | solution.py:20
  44.3 0.0 collective-permute-done.6.rest_2_
  44.3 2.5 %collective-permute-start.10 = (f32[512,128]{1,0:T(8,128)S(1)}, f32[512,128]{1,0:T(8,128)S(1)}, u32[]{:S(2)}, u32[]{:S(2)}) collective-permute-start(f32[512,128]{1,0:T(8,128)S(1)} %collective-permute-done.6.rest_2_), channel_id=1, source_target_pairs={{0,16},{2,18},{4,20},{6,22},{8,24},{10,26},{12,28},{14,30},{16,0},... | collective-permute-start | bytes 786440 | tf_op jit(solution)/shard_map/ppermute | solution.py:20
  46.7 0.0 collective-permute-done.5.rest_1_
  46.8 0.0 collective-permute-start.9
  46.8 0.0 copy-done.5
  46.8 0.0 collective-permute-done.8.rest_4_
  46.8 0.0 collective-permute-done.11.rest_7_
  46.8 1.1 %collective-permute-done.10.rest_6_ = f32[512,128]{1,0:T(8,128)S(1)} collective-permute-done((f32[512,128]{1,0:T(8,128)S(1)}, f32[512,128]{1,0:T(8,128)S(1)}, u32[]{:S(2)}, u32[]{:S(2)}) %collective-permute-start.10) | collective-permute-done | bytes 262176 | tf_op jit(solution)/shard_map/ppermute | solution.py:20
  47.9 0.4 collective-permute-done.9.rest_5_
  48.3 0.0 copy-done.2
  48.3 0.0 copy-done.3
  48.3 0.0 copy-start
  48.3 2.2 %copy-done = bf16[8192,256]{1,0:T(8,128)(2,1)S(1)} copy-done((bf16[8192,256]{1,0:T(8,128)(2,1)S(1)}, bf16[8192,256]{1,0:T(8,128)(2,1)}, u32[]{:S(2)}) %copy-start) | copy-done | bytes 4194328
  50.5 0.0 copy-start.1
  50.5 2.2 %copy-done.1 = bf16[8192,256]{1,0:T(8,128)(2,1)S(1)} copy-done((bf16[8192,256]{1,0:T(8,128)(2,1)S(1)}, bf16[8192,256]{1,0:T(8,128)(2,1)}, u32[]{:S(2)}) %copy-start.1) | copy-done | bytes 4194328
  52.7 9.5 %shard_map.55 = f32[8192,256]{1,0:T(8,128)} custom-call(s32[2048]{0:T(1024)S(1)} %and_add_fusion.slots, s32[16]{0:T(128)S(1)} %copy-done.2, s32[64]{0:T(128)S(1)} %copy-done.3, bf16[8192,256]{1,0:T(8,128)(2,1)S(1)} %copy-done.1, bf16[8192,256]{1,0:T(8,128)(2,1)S(1)} %copy-done, f32[512,128]{1,0:T(8,128)S(1)} %pad_maximum_fusion.rest_0_, ...), custom_call_target="tpu_custom_call" | custom-call | tf_op jit(solution)/shard_map/pallas_call | solution.py:102
  (8 shorter events, 0.1 us)
Async XLA Ops:
  0.0 11.9 %copy-start.4 = (f32[16,256]{1,0:T(8,128)S(1)}, f32[16,256]{1,0:T(8,128)}, u32[]{:S(2)}) copy-start(f32[16,256]{1,0:T(8,128)} %param.6) | copy-start | bytes 49156
  0.0 46.8 %copy-start.5 = (s32[2048]{0:T(1024)S(1)}, s32[2048]{0:T(1024)}, u32[]{:S(2)}) copy-start(s32[2048]{0:T(1024)} %param.9) | copy-start | bytes 24580
  0.0 48.3 %copy-start.2 = (s32[16]{0:T(128)S(1)}, s32[16]{0:T(128)}, u32[]{:S(2)}) copy-start(s32[16]{0:T(128)} %cd_irrep.1) | copy-start | bytes 196
  0.0 48.3 %copy-start.3 = (s32[64]{0:T(128)S(1)}, s32[64]{0:T(128)}, u32[]{:S(2)}) copy-start(s32[64]{0:T(128)} %row_irrep.1) | copy-start | bytes 772
  0.0 11.7 %collective-permute-start = (f32[16,256]{1,0:T(8,128)}, f32[16,256]{1,0:T(8,128)S(1)}, u32[]{:S(2)}, u32[]{:S(2)}) collective-permute-start(f32[16,256]{1,0:T(8,128)} %param.6), channel_id=1, source_target_pairs={{0,1},{1,0},{2,3},{3,2},{4,5},{5,4},{6,7},{7,6},{8,9},{9,8},{10,11... | collective-permute-start | bytes 49160 | tf_op jit(solution)/shard_map/ppermute | solution.py:136
  11.9 6.8 %collective-permute-start.1 = (f32[32,128]{1,0:T(8,128)S(1)}, f32[32,128]{1,0:T(8,128)S(1)}, u32[]{:S(2)}, u32[]{:S(2)}) collective-permute-start(f32[32,128]{1,0:T(8,128)S(1)} %pad_maximum_fusion.4), channel_id=1, source_target_pairs={{0,14},{2,12},{4,10},{6,8},{8,6},{10,4},{12,2},{14,0},{16,30},{18,... | collective-permute-start | bytes 49160 | tf_op jit(solution)/shard_map/ppermute | solution.py:20
  18.7 3.7 %collective-permute-start.2 = (f32[64,128]{1,0:T(8,128)S(1)}, f32[64,128]{1,0:T(8,128)S(1)}, u32[]{:S(2)}, u32[]{:S(2)}) collective-permute-start(f32[64,128]{1,0:T(8,128)S(1)} %pad_maximum_fusion.3), channel_id=1, source_target_pairs={{0,4},{2,6},{4,0},{6,2},{8,12},{10,14},{12,8},{14,10},{16,20},{18,... | collective-permute-start | bytes 98312 | tf_op jit(solution)/shard_map/ppermute | solution.py:20
  22.4 3.1 %collective-permute-start.3 = (f32[128,128]{1,0:T(8,128)S(1)}, f32[128,128]{1,0:T(8,128)S(1)}, u32[]{:S(2)}, u32[]{:S(2)}) collective-permute-start(f32[128,128]{1,0:T(8,128)S(1)} %pad_maximum_fusion.2), channel_id=1, source_target_pairs={{0,192},{2,194},{4,196},{6,198},{8,200},{10,202},{12,204},{14,206}... | collective-permute-start | bytes 196616 | tf_op jit(solution)/shard_map/ppermute | solution.py:20
  25.5 3.9 %collective-permute-start.4 = (f32[256,128]{1,0:T(8,128)S(1)}, f32[256,128]{1,0:T(8,128)S(1)}, u32[]{:S(2)}, u32[]{:S(2)}) collective-permute-start(f32[256,128]{1,0:T(8,128)S(1)} %pad_maximum_fusion.1), channel_id=1, source_target_pairs={{0,2},{2,0},{4,6},{6,4},{8,10},{10,8},{12,14},{14,12},{16,80},{18,... | collective-permute-start | bytes 393224 | tf_op jit(solution)/shard_map/ppermute | solution.py:20
  29.5 10.9 %collective-permute-start.7 = (f32[512,128]{1,0:T(8,128)S(1)}, f32[512,128]{1,0:T(8,128)S(1)}, u32[]{:S(2)}, u32[]{:S(2)}) collective-permute-start(f32[512,128]{1,0:T(8,128)S(1)} %pad_maximum_fusion.rest_0_), channel_id=1, source_target_pairs={{0,96},{2,98},{4,100},{6,102},{8,104},{10,106},{12,108},{14,110},{... | collective-permute-start | bytes 786440 | tf_op jit(solution)/shard_map/ppermute | solution.py:20
  33.6 10.7 %collective-permute-start.6 = (f32[512,128]{1,0:T(8,128)S(1)}, f32[512,128]{1,0:T(8,128)S(1)}, u32[]{:S(2)}, u32[]{:S(2)}) collective-permute-start(f32[512,128]{1,0:T(8,128)S(1)} %pad_maximum_fusion.rest_0_), channel_id=1, source_target_pairs={{0,64},{2,66},{4,68},{6,70},{8,72},{10,74},{12,76},{14,78},{16,208... | collective-permute-start | bytes 786440 | tf_op jit(solution)/shard_map/ppermute | solution.py:20
  33.6 13.1 %collective-permute-start.5 = (f32[512,128]{1,0:T(8,128)S(1)}, f32[512,128]{1,0:T(8,128)S(1)}, u32[]{:S(2)}, u32[]{:S(2)}) collective-permute-start(f32[512,128]{1,0:T(8,128)S(1)} %pad_maximum_fusion.rest_0_), channel_id=1, source_target_pairs={{0,32},{2,34},{4,36},{6,38},{8,40},{10,42},{12,44},{14,46},{16,18}... | collective-permute-start | bytes 786440 | tf_op jit(solution)/shard_map/ppermute | solution.py:20
  34.0 12.8 %collective-permute-start.8 = (f32[512,128]{1,0:T(8,128)S(1)}, f32[512,128]{1,0:T(8,128)S(1)}, u32[]{:S(2)}, u32[]{:S(2)}) collective-permute-start(f32[512,128]{1,0:T(8,128)S(1)} %pad_maximum_fusion.rest_0_), channel_id=1, source_target_pairs={{0,16},{2,18},{4,20},{6,22},{8,24},{10,26},{12,28},{14,30},{16,0},... | collective-permute-start | bytes 786440 | tf_op jit(solution)/shard_map/ppermute | solution.py:20
  40.4 6.4 %collective-permute-start.11 = (f32[512,128]{1,0:T(8,128)S(1)}, f32[512,128]{1,0:T(8,128)S(1)}, u32[]{:S(2)}, u32[]{:S(2)}) collective-permute-start(f32[512,128]{1,0:T(8,128)S(1)} %collective-permute-done.7.rest_3_), channel_id=1, source_target_pairs={{0,16},{2,18},{4,20},{6,22},{8,24},{10,26},{12,28},{14,30},{16,0},... | collective-permute-start | bytes 786440 | tf_op jit(solution)/shard_map/ppermute | solution.py:20
  44.3 3.6 %collective-permute-start.10 = (f32[512,128]{1,0:T(8,128)S(1)}, f32[512,128]{1,0:T(8,128)S(1)}, u32[]{:S(2)}, u32[]{:S(2)}) collective-permute-start(f32[512,128]{1,0:T(8,128)S(1)} %collective-permute-done.6.rest_2_), channel_id=1, source_target_pairs={{0,16},{2,18},{4,20},{6,22},{8,24},{10,26},{12,28},{14,30},{16,0},... | collective-permute-start | bytes 786440 | tf_op jit(solution)/shard_map/ppermute | solution.py:20
  46.8 1.5 %collective-permute-start.9 = (f32[512,128]{1,0:T(8,128)S(1)}, f32[512,128]{1,0:T(8,128)S(1)}, u32[]{:S(2)}, u32[]{:S(2)}) collective-permute-start(f32[512,128]{1,0:T(8,128)S(1)} %collective-permute-done.5.rest_1_), channel_id=1, source_target_pairs={{0,16},{2,18},{4,20},{6,22},{8,24},{10,26},{12,28},{14,30},{16,0},... | collective-permute-start | bytes 786440 | tf_op jit(solution)/shard_map/ppermute | solution.py:20
  48.3 2.2 %copy-start = (bf16[8192,256]{1,0:T(8,128)(2,1)S(1)}, bf16[8192,256]{1,0:T(8,128)(2,1)}, u32[]{:S(2)}) copy-start(bf16[8192,256]{1,0:T(8,128)(2,1)} %get-tuple-element.9.a_lo) | copy-start | bytes 12582916
  50.5 2.2 %copy-start.1 = (bf16[8192,256]{1,0:T(8,128)(2,1)S(1)}, bf16[8192,256]{1,0:T(8,128)(2,1)}, u32[]{:S(2)}) copy-start(bf16[8192,256]{1,0:T(8,128)(2,1)} %get-tuple-element.8.a_hi) | copy-start | bytes 12582916

commit v3 on v2

v3 whole, which is shorter than its diff:
```python
import jax
import jax.numpy as jnp
from jax import lax
from jax.experimental import pallas as pl
from jax.experimental.pallas import tpu as pltpu
from jax.sharding import PartitionSpec as P

CORE = 8
Z1, Z2, Z6, X1, Y1, Y3 = 1, 2, 6, 16, 32, 96
STEPS = ((Z6, Z6), (Z2, Z2), (Y3, X1), (Z1, Y1), (X1, Z1), (Y1, Y3))

CHUNK = 512
STRIDE = 2048


def trade(block, masks):
    route = [(i, i ^ masks[i // CORE % 2]) for i in range(128)]
    return lax.ppermute(block, ("aa", "ba"), [(i, j) for i, j in route if i != j])


def trade_raw(amplitudes, masks):
    route = [(i, i ^ masks[i // 2 // CORE % 2]) for i in range(256)]
    return lax.ppermute(amplitudes, ("aa", "ba", "ao"), [(i, j) for i, j in route if i != j])


def slot_bits(core):
    masks = [step[core] for step in STEPS]
    source_of = {}
    for slot in range(64):
        source = 0
        for bit, mask in enumerate(masks):
            if slot >> bit & 1:
                source ^= mask
        source_of[source] = slot
    return [0 if 1 << bit == CORE else source_of[1 << bit] for bit in range(7)]


def ladder_kernel(labels, integrals, *rest):
    pieces, (out, block_of, a_buf, gathered, picked, high, low, o_buf, a_sem, o_sem) = rest[:8], rest[8:]
    rows = out.shape[0]
    block = picked.shape[0] // 32
    size = pieces[0].shape[0]
    pairs, row_blocks = 16 * block, rows // block

    def fetch(i):
        at = pl.ds(i * STRIDE, STRIDE)
        return pltpu.make_async_copy(integrals.at[at], a_buf.at[at], a_sem.at[i])

    def flush(i):
        at = pl.ds(i * CHUNK, CHUNK)
        return pltpu.make_async_copy(o_buf.at[at], out.at[at], o_sem.at[i])

    for i in range(rows // STRIDE):
        fetch(i).start()
    for i, piece in enumerate(pieces):
        gathered[i * size : (i + 1) * size, :] = piece[...]
    for s in range(16):
        block_of[s] = -1
    for b in range(16):
        s = labels[pairs + row_blocks + b]
        half = jnp.where(block_of[2 * s] < 0, 0, 1)
        block_of[2 * s + half] = b

    def pick(q, carry):
        base = block_of[q] * block

        for j in range(block):
            row = pl.multiple_of(labels[base + j], 2)
            picked[pl.ds(pl.multiple_of((q * block + j) * 2, 2), 2), :] = gathered[pl.ds(row, 2), :]
        return carry

    lax.fori_loop(0, 16, pick, 0)

    def split(s, carry):
        for c in range(2):
            v = picked[pl.ds(s * 4 * block + c, 2 * block, stride=2), :]
            hi = v.astype(jnp.bfloat16)
            high[s, :, c * 128 : c * 128 + 128] = hi
            low[s, :, c * 128 : c * 128 + 128] = (v - hi.astype(jnp.float32)).astype(jnp.bfloat16)
        return carry

    lax.fori_loop(0, 8, split, 0)

    def step(i, carry):
        fetch(i).wait()
        for k in range(STRIDE // block):
            at = pl.ds(pl.multiple_of(i * STRIDE + k * block, block), block)
            s = labels[pairs + i * (STRIDE // block) + k]
            a, b_hi = a_buf[at, :], high[s]
            a_hi = a.astype(jnp.bfloat16)
            a_lo = (a - a_hi.astype(jnp.float32)).astype(jnp.bfloat16)
            left = jnp.concatenate([a_hi, a_lo, a_hi], axis=1)
            right = jnp.concatenate([low[s], b_hi, b_hi], axis=0)
            o_buf[at, :] = jnp.dot(left, right, preferred_element_type=jnp.float32)
            done = (k + 1) * block - CHUNK
            if done > 0 and done % CHUNK == 0:
                flush(i * (STRIDE // CHUNK) + done // CHUNK - 1).start()
        flush((i + 1) * (STRIDE // CHUNK) - 1).start()
        return carry

    lax.fori_loop(0, rows // STRIDE, step, 0)
    for i in range(rows // CHUNK):
        flush(i).wait()


def ladder(labels, integrals, pieces):
    rows = integrals.shape[0]
    smem = pl.BlockSpec(memory_space=pltpu.SMEM)
    vmem = pl.BlockSpec(memory_space=pltpu.VMEM)
    hbm = pl.BlockSpec(memory_space=pl.ANY)
    return pl.pallas_call(
        ladder_kernel,
        out_shape=jax.ShapeDtypeStruct((rows, 256), jnp.float32),
        in_specs=[smem, hbm] + [vmem] * len(pieces),
        out_specs=hbm,
        scratch_shapes=[
            pltpu.SMEM((16,), jnp.int32),
            pltpu.VMEM((rows, 256), jnp.float32),
            pltpu.VMEM((4096, 128), jnp.float32),
            pltpu.VMEM((4096, 128), jnp.float32),
            pltpu.VMEM((8, 256, 256), jnp.bfloat16),
            pltpu.VMEM((8, 256, 256), jnp.bfloat16),
            pltpu.VMEM((rows, 256), jnp.float32),
            pltpu.SemaphoreType.DMA((rows // STRIDE,)),
            pltpu.SemaphoreType.DMA((rows // CHUNK,)),
        ],
        compiler_params=pltpu.CompilerParams(vmem_limit_bytes=48 << 20),
    )(labels, integrals, *pieces)


def on_device(integrals, amplitudes, row_irrep, cd_irrep, cd_order):
    me = lax.axis_index(("aa", "ba"))
    source = cd_order >> 4
    relative = source ^ me
    slot = (relative >> 3 & 1) << 6
    for bit, (zero, one) in enumerate(zip(slot_bits(0), slot_bits(1))):
        image = jnp.where(source >> 3 & 1 == 1, one, zero)
        slot = slot ^ jnp.where(relative >> bit & 1 == 1, image, 0)
    labels = jnp.concatenate([slot * 32 + (cd_order & 15) * 2, row_irrep, cd_irrep])

    parity = (1 - 2 * lax.axis_index("ao")).astype(jnp.float32)
    partner = trade_raw(amplitudes, (1, 1))
    block = (partner[:, ::-1] + parity * amplitudes).reshape(-1, 128)
    for masks in STEPS[0:-2]:
        block = lax.optimization_barrier(jnp.concatenate([block, trade(block, masks)]))
    block, labels = lax.optimization_barrier((block, labels))
    a, b = STEPS[-2:]
    both = tuple(p ^ q for p, q in zip(a, b))
    pieces = [block, trade(block, a), trade(block, b), trade(block, both)]
    pieces += [trade(piece, (CORE, CORE)) for piece in pieces]
    return ladder(labels, integrals, pieces)


def solution(mesh):
    placed = (P(("aa", "ba"), None), P(("aa", "ba"), "ao"), P(("aa", "ba")), P(), P())
    return jax.shard_map(
        on_device, mesh=mesh, in_specs=placed, out_specs=P(("aa", "ba"), "ao"), check_vma=False
    )
```

time: 62.4 us -> 52.7 us (0.84)
  other arithmetic: 8.13 us -> 1.48 us
  local copies, waits for them, and re-layouts: 4.55 us -> 0.9 us
  starting transfers between devices: 30.4 us -> 32.2 us
  Pallas kernels: 9.52 us -> 8.09 us
    convert_element_type x1 -> x0, other arithmetic: 8.07 us -> none  [on_device(): a_lo = (integrals - rounded).astype(jnp.bfloat16)]
    unnamed x12 -> x0, local copies, waits for them, and re-layouts: 4.39 us -> none
    ppermute x12, starting transfers between devices: 30.4 us -> 32.2 us  [the longest x11 28.6 us: trade(): lax.ppermute(block, ('aa', 'ba'), [(i, j) for i, j in route if i != j])]
    pallas_call x1, Pallas kernels: 9.52 us -> 8.09 us  [ladder(): pl.pallas_call(ladder_kernel, out_shape=jax.ShapeDtypeStruct((rows, 256),...]
    add x2, other arithmetic: 0.02 us -> 1.44 us  [the longest x1 0.73 us: on_device(): block = (partner[:, ::-1] + parity * amplitudes).reshape(-1, 128)]
    concatenate x0 -> x1, local copies, waits for them, and re-layouts: none -> 0.75 us  [on_device(): jnp.concatenate([slot * 32 + (cd_order & 15) * 2, row_irrep, cd_irrep])]
  transfers between devices with their start and end apart: 12 -> 12, of which waited for: 6 -> 7; matrix products, arithmetic and copies ran while one was open for 13% -> 3% of each run, Pallas kernels for 0% -> 0%
where the time goes in v3:
time: 52.7 us; the launch traced here: 52.4 us
  starting transfers between devices  32.2 us (61%)
  waiting for transfers between devices  9.74 us (18%)
  Pallas kernels  8.09 us (15%)
  other arithmetic  1.48 us (3%)
  local copies, waits for them, and re-layouts  0.9 us (2%)
    ppermute x11, starting transfers between devices, trade(): lax.ppermute(block, ('aa', 'ba'), [(i, j) for i, j in route if i != j])  28.6 us
    ppermute x11, waiting for transfers between devices, trade(): lax.ppermute(block, ('aa', 'ba'), [(i, j) for i, j in route if i != j])  8.4 us
    pallas_call x1, Pallas kernels, ladder(): pl.pallas_call(ladder_kernel, out_shape=jax.ShapeDtypeStruct((rows, 256),...  8.09 us
    ppermute x1, starting transfers between devices, trade_raw(): lax.ppermute(amplitudes, ('aa', 'ba', 'ao'), [(i, j) for i, j in route if...  3.57 us
    ppermute x1, waiting for transfers between devices, trade_raw(): lax.ppermute(amplitudes, ('aa', 'ba', 'ao'), [(i, j) for i, j in route if...  1.34 us
  transfers between devices with their start and end apart: 12, of which 7 were waited for; matrix products, arithmetic and copies ran while one was open for 3% of the time, Pallas kernels for 0%

profile of v3, /device:TPU:1, one launch (start us, length us, event | category | flops | bytes accessed | tf_op | source)
XLA Modules:
  0.0 52.4 jit_solution(13726016008269249861)
XLA Ops:
  0.0 3.6 %collective-permute-start = (f32[16,256]{1,0:T(8,128)}, f32[16,256]{1,0:T(8,128)S(1)}, u32[]{:S(2)}, u32[]{:S(2)}) collective-permute-start(f32[16,256]{1,0:T(8,128)} %param.6), channel_id=1, source_target_pairs={{0,1},{1,0},{2,3},{3,2},{4,5},{5,4},{6,7},{7,6},{8,9},{9,8},{10,11... | collective-permute-start | bytes 49160 | tf_op jit(solution)/shard_map/ppermute | solution.py:23
  3.6 1.3 %collective-permute-done = f32[16,256]{1,0:T(8,128)S(1)} collective-permute-done((f32[16,256]{1,0:T(8,128)}, f32[16,256]{1,0:T(8,128)S(1)}, u32[]{:S(2)}, u32[]{:S(2)}) %collective-permute-start) | collective-permute-done | bytes 16416 | tf_op jit(solution)/shard_map/ppermute | solution.py:23
  4.9 0.1 rev.3
  5.1 0.7 %multiply_add_fusion = f32[16,256]{1,0:T(8,128)S(1)} fusion(f32[16,256]{1,0:T(8,128)S(1)} %rev.3, f32[16,256]{1,0:T(8,128)} %param.6, f32[]{:T(128)S(6)} %convert_element_type.3), kind=kLoop, calls=%fused_computation.4 | loop fusion | flops 8192 | bytes 49156 | tf_op jit(solution)/shard_map/add | solution.py:143
  5.8 6.2 %collective-permute-start.1 = (f32[32,128]{1,0:T(8,128)S(1)}, f32[32,128]{1,0:T(8,128)S(1)}, u32[]{:S(2)}, u32[]{:S(2)}) collective-permute-start(f32[32,128]{1,0:T(8,128)S(1)} %reshape.3), channel_id=1, source_target_pairs={{0,12},{2,14},{4,8},{6,10},{8,4},{10,6},{12,0},{14,2},{16,28},{18,... | collective-permute-start | bytes 49160 | tf_op jit(solution)/shard_map/ppermute | solution.py:18
  12.0 1.1 %collective-permute-done.1 = f32[32,128]{1,0:T(8,128)S(1)} collective-permute-done((f32[32,128]{1,0:T(8,128)S(1)}, f32[32,128]{1,0:T(8,128)S(1)}, u32[]{:S(2)}, u32[]{:S(2)}) %collective-permute-start.1) | collective-permute-done | bytes 16416 | tf_op jit(solution)/shard_map/ppermute | solution.py:18
  13.2 1.2 %collective-permute-start.2 = (f32[64,128]{1,0:T(8,128)S(1)}, f32[64,128]{1,0:T(8,128)S(1)}, u32[]{:S(2)}, u32[]{:S(2)}) collective-permute-start(f32[64,128]{1,0:T(8,128)S(1)} %pad_maximum_fusion.3), channel_id=1, source_target_pairs={{0,4},{2,6},{4,0},{6,2},{8,12},{10,14},{12,8},{14,10},{16,20},{18,... | collective-permute-start | bytes 98312 | tf_op jit(solution)/shard_map/ppermute | solution.py:18
  14.3 2.5 %collective-permute-done.2 = f32[64,128]{1,0:T(8,128)S(1)} collective-permute-done((f32[64,128]{1,0:T(8,128)S(1)}, f32[64,128]{1,0:T(8,128)S(1)}, u32[]{:S(2)}, u32[]{:S(2)}) %collective-permute-start.2) | collective-permute-done | bytes 32800 | tf_op jit(solution)/shard_map/ppermute | solution.py:18
  16.8 1.2 %collective-permute-start.3 = (f32[128,128]{1,0:T(8,128)S(1)}, f32[128,128]{1,0:T(8,128)S(1)}, u32[]{:S(2)}, u32[]{:S(2)}) collective-permute-start(f32[128,128]{1,0:T(8,128)S(1)} %pad_maximum_fusion.2), channel_id=1, source_target_pairs={{0,192},{2,194},{4,196},{6,198},{8,200},{10,202},{12,204},{14,206}... | collective-permute-start | bytes 196616 | tf_op jit(solution)/shard_map/ppermute | solution.py:18
  18.0 2.2 %collective-permute-done.3 = f32[128,128]{1,0:T(8,128)S(1)} collective-permute-done((f32[128,128]{1,0:T(8,128)S(1)}, f32[128,128]{1,0:T(8,128)S(1)}, u32[]{:S(2)}, u32[]{:S(2)}) %collective-permute-start.3) | collective-permute-done | bytes 65568 | tf_op jit(solution)/shard_map/ppermute | solution.py:18
  20.3 1.4 %collective-permute-start.4 = (f32[256,128]{1,0:T(8,128)S(1)}, f32[256,128]{1,0:T(8,128)S(1)}, u32[]{:S(2)}, u32[]{:S(2)}) collective-permute-start(f32[256,128]{1,0:T(8,128)S(1)} %pad_maximum_fusion.1), channel_id=1, source_target_pairs={{0,2},{2,0},{4,6},{6,4},{8,10},{10,8},{12,14},{14,12},{16,80},{18,... | collective-permute-start | bytes 393224 | tf_op jit(solution)/shard_map/ppermute | solution.py:18
  21.6 0.7 %multiply_add_fusion.1 = s32[2048]{0:T(1024)S(1)} fusion(s32[2048]{0:T(1024)} %param.9, s32[]{:T(128)S(6)} %add.10), kind=kLoop, calls=%fused_computation.5 | loop fusion | flops 94208 | bytes 16388 | tf_op jit(solution)/shard_map/add | solution.py:139
  22.4 0.7 %concatenate.19.labels = s32[2128]{0:T(1024)S(1)} concatenate(s32[2048]{0:T(1024)S(1)} %multiply_add_fusion.1, s32[64]{0:T(128)} %param.7, s32[16]{0:T(128)} %param.8), dimensions={0} | concatenate | bytes 17024 | tf_op jit(solution)/shard_map/concatenate | solution.py:139
  23.1 1.1 %collective-permute-done.4 = f32[256,128]{1,0:T(8,128)S(1)} collective-permute-done((f32[256,128]{1,0:T(8,128)S(1)}, f32[256,128]{1,0:T(8,128)S(1)}, u32[]{:S(2)}, u32[]{:S(2)}) %collective-permute-start.4) | collective-permute-done | bytes 131104 | tf_op jit(solution)/shard_map/ppermute | solution.py:18
  24.2 3.3 %collective-permute-start.7 = (f32[512,128]{1,0:T(8,128)S(1)}, f32[512,128]{1,0:T(8,128)S(1)}, u32[]{:S(2)}, u32[]{:S(2)}) collective-permute-start(f32[512,128]{1,0:T(8,128)S(1)} %pad_maximum_fusion.rest_0_), channel_id=1, source_target_pairs={{0,96},{2,98},{4,100},{6,102},{8,104},{10,106},{12,108},{14,110},{... | collective-permute-start | bytes 786440 | tf_op jit(solution)/shard_map/ppermute | solution.py:18
  27.5 0.0 collective-permute-start.6
  27.5 0.7 %collective-permute-start.5 = (f32[512,128]{1,0:T(8,128)S(1)}, f32[512,128]{1,0:T(8,128)S(1)}, u32[]{:S(2)}, u32[]{:S(2)}) collective-permute-start(f32[512,128]{1,0:T(8,128)S(1)} %pad_maximum_fusion.rest_0_), channel_id=1, source_target_pairs={{0,32},{2,34},{4,36},{6,38},{8,40},{10,42},{12,44},{14,46},{16,18}... | collective-permute-start | bytes 786440 | tf_op jit(solution)/shard_map/ppermute | solution.py:18
  28.2 8.0 %collective-permute-start.8 = (f32[512,128]{1,0:T(8,128)S(1)}, f32[512,128]{1,0:T(8,128)S(1)}, u32[]{:S(2)}, u32[]{:S(2)}) collective-permute-start(f32[512,128]{1,0:T(8,128)S(1)} %pad_maximum_fusion.rest_0_), channel_id=1, source_target_pairs={{0,16},{2,18},{4,20},{6,22},{8,24},{10,26},{12,28},{14,30},{16,0},... | collective-permute-start | bytes 786440 | tf_op jit(solution)/shard_map/ppermute | solution.py:18
  36.2 0.0 collective-permute-done.7.rest_3_
  36.2 3.9 %collective-permute-start.11 = (f32[512,128]{1,0:T(8,128)S(1)}, f32[512,128]{1,0:T(8,128)S(1)}, u32[]{:S(2)}, u32[]{:S(2)}) collective-permute-start(f32[512,128]{1,0:T(8,128)S(1)} %collective-permute-done.7.rest_3_), channel_id=1, source_target_pairs={{0,16},{2,18},{4,20},{6,22},{8,24},{10,26},{12,28},{14,30},{16,0},... | collective-permute-start | bytes 786440 | tf_op jit(solution)/shard_map/ppermute | solution.py:18
  40.1 0.0 collective-permute-done.6.rest_2_
  40.1 2.7 %collective-permute-start.10 = (f32[512,128]{1,0:T(8,128)S(1)}, f32[512,128]{1,0:T(8,128)S(1)}, u32[]{:S(2)}, u32[]{:S(2)}) collective-permute-start(f32[512,128]{1,0:T(8,128)S(1)} %collective-permute-done.6.rest_2_), channel_id=1, source_target_pairs={{0,16},{2,18},{4,20},{6,22},{8,24},{10,26},{12,28},{14,30},{16,0},... | collective-permute-start | bytes 786440 | tf_op jit(solution)/shard_map/ppermute | solution.py:18
  42.8 0.0 collective-permute-done.5.rest_1_
  42.8 0.0 collective-permute-start.9
  42.8 0.0 collective-permute-done.8.rest_4_
  42.8 0.0 collective-permute-done.11.rest_7_
  42.8 1.1 %collective-permute-done.10.rest_6_ = f32[512,128]{1,0:T(8,128)S(1)} collective-permute-done((f32[512,128]{1,0:T(8,128)S(1)}, f32[512,128]{1,0:T(8,128)S(1)}, u32[]{:S(2)}, u32[]{:S(2)}) %collective-permute-start.10) | collective-permute-done | bytes 262176 | tf_op jit(solution)/shard_map/ppermute | solution.py:18
  44.0 0.4 collective-permute-done.9.rest_5_
  44.3 8.1 %shard_map.55 = f32[8192,256]{1,0:T(8,128)} custom-call(s32[2128]{0:T(1024)S(1)} %concatenate.19.labels, f32[8192,256]{1,0:T(8,128)} %integrals.1, f32[512,128]{1,0:T(8,128)S(1)} %pad_maximum_fusion.rest_0_, f32[512,128]{1,0:T(8,128)S(1)} %collective-permute-done.5.rest_1_, f32[512,128]{1,0:T(8,128)S(1)} %collective-permute-done.6.rest_2_, ...), custom_call_target="tpu_custom_call" | custom-call | tf_op jit(solution)/shard_map/pallas_call | solution.py:111
  (5 shorter events, 0.0 us)
Async XLA Ops:
  0.0 4.9 %collective-permute-start = (f32[16,256]{1,0:T(8,128)}, f32[16,256]{1,0:T(8,128)S(1)}, u32[]{:S(2)}, u32[]{:S(2)}) collective-permute-start(f32[16,256]{1,0:T(8,128)} %param.6), channel_id=1, source_target_pairs={{0,1},{1,0},{2,3},{3,2},{4,5},{5,4},{6,7},{7,6},{8,9},{9,8},{10,11... | collective-permute-start | bytes 49160 | tf_op jit(solution)/shard_map/ppermute | solution.py:23
  5.8 7.4 %collective-permute-start.1 = (f32[32,128]{1,0:T(8,128)S(1)}, f32[32,128]{1,0:T(8,128)S(1)}, u32[]{:S(2)}, u32[]{:S(2)}) collective-permute-start(f32[32,128]{1,0:T(8,128)S(1)} %reshape.3), channel_id=1, source_target_pairs={{0,12},{2,14},{4,8},{6,10},{8,4},{10,6},{12,0},{14,2},{16,28},{18,... | collective-permute-start | bytes 49160 | tf_op jit(solution)/shard_map/ppermute | solution.py:18
  13.2 3.7 %collective-permute-start.2 = (f32[64,128]{1,0:T(8,128)S(1)}, f32[64,128]{1,0:T(8,128)S(1)}, u32[]{:S(2)}, u32[]{:S(2)}) collective-permute-start(f32[64,128]{1,0:T(8,128)S(1)} %pad_maximum_fusion.3), channel_id=1, source_target_pairs={{0,4},{2,6},{4,0},{6,2},{8,12},{10,14},{12,8},{14,10},{16,20},{18,... | collective-permute-start | bytes 98312 | tf_op jit(solution)/shard_map/ppermute | solution.py:18
  16.8 3.4 %collective-permute-start.3 = (f32[128,128]{1,0:T(8,128)S(1)}, f32[128,128]{1,0:T(8,128)S(1)}, u32[]{:S(2)}, u32[]{:S(2)}) collective-permute-start(f32[128,128]{1,0:T(8,128)S(1)} %pad_maximum_fusion.2), channel_id=1, source_target_pairs={{0,192},{2,194},{4,196},{6,198},{8,200},{10,202},{12,204},{14,206}... | collective-permute-start | bytes 196616 | tf_op jit(solution)/shard_map/ppermute | solution.py:18
  20.3 3.9 %collective-permute-start.4 = (f32[256,128]{1,0:T(8,128)S(1)}, f32[256,128]{1,0:T(8,128)S(1)}, u32[]{:S(2)}, u32[]{:S(2)}) collective-permute-start(f32[256,128]{1,0:T(8,128)S(1)} %pad_maximum_fusion.1), channel_id=1, source_target_pairs={{0,2},{2,0},{4,6},{6,4},{8,10},{10,8},{12,14},{14,12},{16,80},{18,... | collective-permute-start | bytes 393224 | tf_op jit(solution)/shard_map/ppermute | solution.py:18
  24.2 12.0 %collective-permute-start.7 = (f32[512,128]{1,0:T(8,128)S(1)}, f32[512,128]{1,0:T(8,128)S(1)}, u32[]{:S(2)}, u32[]{:S(2)}) collective-permute-start(f32[512,128]{1,0:T(8,128)S(1)} %pad_maximum_fusion.rest_0_), channel_id=1, source_target_pairs={{0,96},{2,98},{4,100},{6,102},{8,104},{10,106},{12,108},{14,110},{... | collective-permute-start | bytes 786440 | tf_op jit(solution)/shard_map/ppermute | solution.py:18
  27.5 12.6 %collective-permute-start.6 = (f32[512,128]{1,0:T(8,128)S(1)}, f32[512,128]{1,0:T(8,128)S(1)}, u32[]{:S(2)}, u32[]{:S(2)}) collective-permute-start(f32[512,128]{1,0:T(8,128)S(1)} %pad_maximum_fusion.rest_0_), channel_id=1, source_target_pairs={{0,64},{2,66},{4,68},{6,70},{8,72},{10,74},{12,76},{14,78},{16,208... | collective-permute-start | bytes 786440 | tf_op jit(solution)/shard_map/ppermute | solution.py:18
  27.5 15.3 %collective-permute-start.5 = (f32[512,128]{1,0:T(8,128)S(1)}, f32[512,128]{1,0:T(8,128)S(1)}, u32[]{:S(2)}, u32[]{:S(2)}) collective-permute-start(f32[512,128]{1,0:T(8,128)S(1)} %pad_maximum_fusion.rest_0_), channel_id=1, source_target_pairs={{0,32},{2,34},{4,36},{6,38},{8,40},{10,42},{12,44},{14,46},{16,18}... | collective-permute-start | bytes 786440 | tf_op jit(solution)/shard_map/ppermute | solution.py:18
  28.2 14.6 %collective-permute-start.8 = (f32[512,128]{1,0:T(8,128)S(1)}, f32[512,128]{1,0:T(8,128)S(1)}, u32[]{:S(2)}, u32[]{:S(2)}) collective-permute-start(f32[512,128]{1,0:T(8,128)S(1)} %pad_maximum_fusion.rest_0_), channel_id=1, source_target_pairs={{0,16},{2,18},{4,20},{6,22},{8,24},{10,26},{12,28},{14,30},{16,0},... | collective-permute-start | bytes 786440 | tf_op jit(solution)/shard_map/ppermute | solution.py:18
  36.2 6.6 %collective-permute-start.11 = (f32[512,128]{1,0:T(8,128)S(1)}, f32[512,128]{1,0:T(8,128)S(1)}, u32[]{:S(2)}, u32[]{:S(2)}) collective-permute-start(f32[512,128]{1,0:T(8,128)S(1)} %collective-permute-done.7.rest_3_), channel_id=1, source_target_pairs={{0,16},{2,18},{4,20},{6,22},{8,24},{10,26},{12,28},{14,30},{16,0},... | collective-permute-start | bytes 786440 | tf_op jit(solution)/shard_map/ppermute | solution.py:18
  40.1 3.9 %collective-permute-start.10 = (f32[512,128]{1,0:T(8,128)S(1)}, f32[512,128]{1,0:T(8,128)S(1)}, u32[]{:S(2)}, u32[]{:S(2)}) collective-permute-start(f32[512,128]{1,0:T(8,128)S(1)} %collective-permute-done.6.rest_2_), channel_id=1, source_target_pairs={{0,16},{2,18},{4,20},{6,22},{8,24},{10,26},{12,28},{14,30},{16,0},... | collective-permute-start | bytes 786440 | tf_op jit(solution)/shard_map/ppermute | solution.py:18
  42.8 1.5 %collective-permute-start.9 = (f32[512,128]{1,0:T(8,128)S(1)}, f32[512,128]{1,0:T(8,128)S(1)}, u32[]{:S(2)}, u32[]{:S(2)}) collective-permute-start(f32[512,128]{1,0:T(8,128)S(1)} %collective-permute-done.5.rest_1_), channel_id=1, source_target_pairs={{0,16},{2,18},{4,20},{6,22},{8,24},{10,26},{12,28},{14,30},{16,0},... | collective-permute-start | bytes 786440 | tf_op jit(solution)/shard_map/ppermute | solution.py:18

commit v4 on v3

--- a/solution.py
+++ b/solution.py
@@ -36,7 +36,7 @@
 
 
 def ladder_kernel(labels, integrals, *rest):
-    pieces, (out, block_of, a_buf, gathered, picked, high, low, o_buf, a_sem, o_sem) = rest[:8], rest[8:]
+    pieces, (out, block_of, a_buf, gathered, picked, high, low, o_buf, a_sem, o_sem) = rest[:-10], rest[-10:]
     rows = out.shape[0]
     block = picked.shape[0] // 32
     size = pieces[0].shape[0]
@@ -141,12 +141,16 @@
     parity = (1 - 2 * lax.axis_index("ao")).astype(jnp.float32)
     partner = trade_raw(amplitudes, (1, 1))
     block = (partner[:, ::-1] + parity * amplitudes).reshape(-1, 128)
-    for masks in STEPS[0:-2]:
+    for masks in STEPS[:-3]:
         block = lax.optimization_barrier(jnp.concatenate([block, trade(block, masks)]))
     block, labels = lax.optimization_barrier((block, labels))
     a, b = STEPS[-2:]
     both = tuple(p ^ q for p, q in zip(a, b))
-    pieces = [block, trade(block, a), trade(block, b), trade(block, both)]
+    later = trade(block, STEPS[-3])
+    early = [trade(block, masks) for masks in (a, b, both)]
+    late = [trade(later, masks) for masks in (a, b, both)]
+    *early, late[2] = lax.optimization_barrier((*early, late[2]))
+    pieces = [block, later] + [piece for pair in zip(early, late) for piece in pair]
     pieces += [trade(piece, (CORE, CORE)) for piece in pieces]
     return ladder(labels, integrals, pieces)
 

time: 52.7 us -> 50.1 us (0.951)
  waiting for transfers between devices: 9.74 us -> 6.73 us
    ppermute x11 -> x18, waiting for transfers between devices: 8.4 us -> 5.4 us  [trade(): lax.ppermute(block, ('aa', 'ba'), [(i, j) for i, j in route if i != j])]
    ppermute x11 -> x18, starting transfers between devices: 28.6 us -> 28.8 us  [trade(): lax.ppermute(block, ('aa', 'ba'), [(i, j) for i, j in route if i != j])]
  transfers between devices with their start and end apart: 12 -> 19, of which waited for: 7 -> 7; matrix products, arithmetic and copies ran while one was open for 3% -> 3% of each run, Pallas kernels for 0% -> 0%
where the time goes in v4:
time: 50.1 us; the launch traced here: 49.6 us
  starting transfers between devices  32.4 us (65%)
  Pallas kernels  8.09 us (16%)
  waiting for transfers between devices  6.73 us (13%)
  other arithmetic  1.46 us (3%)
  local copies, waits for them, and re-layouts  0.9 us (2%)
    ppermute x18, starting transfers between devices, trade(): lax.ppermute(block, ('aa', 'ba'), [(i, j) for i, j in route if i != j])  28.8 us
    pallas_call x1, Pallas kernels, ladder(): pl.pallas_call(ladder_kernel, out_shape=jax.ShapeDtypeStruct((rows, 256),...  8.09 us
    ppermute x18, waiting for transfers between devices, trade(): lax.ppermute(block, ('aa', 'ba'), [(i, j) for i, j in route if i != j])  5.4 us
    ppermute x1, starting transfers between devices, trade_raw(): lax.ppermute(amplitudes, ('aa', 'ba', 'ao'), [(i, j) for i, j in route if...  3.57 us
    ppermute x1, waiting for transfers between devices, trade_raw(): lax.ppermute(amplitudes, ('aa', 'ba', 'ao'), [(i, j) for i, j in route if...  1.34 us
  transfers between devices with their start and end apart: 19, of which 7 were waited for; matrix products, arithmetic and copies ran while one was open for 3% of the time, Pallas kernels for 0%

profile of v4, /device:TPU:1, one launch (start us, length us, event | category | flops | bytes accessed | tf_op | source)
XLA Modules:
  0.0 49.6 jit_solution(6969276735194057529)
XLA Ops:
  0.0 3.6 %collective-permute-start = (f32[16,256]{1,0:T(8,128)}, f32[16,256]{1,0:T(8,128)S(1)}, u32[]{:S(2)}, u32[]{:S(2)}) collective-permute-start(f32[16,256]{1,0:T(8,128)} %param.6), channel_id=1, source_target_pairs={{0,1},{1,0},{2,3},{3,2},{4,5},{5,4},{6,7},{7,6},{8,9},{9,8},{10,11... | collective-permute-start | bytes 49160 | tf_op jit(solution)/shard_map/ppermute | solution.py:23
  3.6 1.3 %collective-permute-done = f32[16,256]{1,0:T(8,128)S(1)} collective-permute-done((f32[16,256]{1,0:T(8,128)}, f32[16,256]{1,0:T(8,128)S(1)}, u32[]{:S(2)}, u32[]{:S(2)}) %collective-permute-start) | collective-permute-done | bytes 16416 | tf_op jit(solution)/shard_map/ppermute | solution.py:23
  4.9 0.1 rev.3
  5.1 0.7 %multiply_add_fusion = f32[16,256]{1,0:T(8,128)S(1)} fusion(f32[16,256]{1,0:T(8,128)S(1)} %rev.3, f32[16,256]{1,0:T(8,128)} %param.6, f32[]{:T(128)S(6)} %convert_element_type.3), kind=kLoop, calls=%fused_computation.3 | loop fusion | flops 8192 | bytes 49156 | tf_op jit(solution)/shard_map/add | solution.py:143
  5.8 6.2 %collective-permute-start.1 = (f32[32,128]{1,0:T(8,128)S(1)}, f32[32,128]{1,0:T(8,128)S(1)}, u32[]{:S(2)}, u32[]{:S(2)}) collective-permute-start(f32[32,128]{1,0:T(8,128)S(1)} %reshape.3), channel_id=1, source_target_pairs={{0,12},{2,14},{4,8},{6,10},{8,4},{10,6},{12,0},{14,2},{16,28},{18,... | collective-permute-start | bytes 49160 | tf_op jit(solution)/shard_map/ppermute | solution.py:18
  12.0 1.1 %collective-permute-done.1 = f32[32,128]{1,0:T(8,128)S(1)} collective-permute-done((f32[32,128]{1,0:T(8,128)S(1)}, f32[32,128]{1,0:T(8,128)S(1)}, u32[]{:S(2)}, u32[]{:S(2)}) %collective-permute-start.1) | collective-permute-done | bytes 16416 | tf_op jit(solution)/shard_map/ppermute | solution.py:18
  13.2 1.2 %collective-permute-start.2 = (f32[64,128]{1,0:T(8,128)S(1)}, f32[64,128]{1,0:T(8,128)S(1)}, u32[]{:S(2)}, u32[]{:S(2)}) collective-permute-start(f32[64,128]{1,0:T(8,128)S(1)} %pad_maximum_fusion.2), channel_id=1, source_target_pairs={{0,4},{2,6},{4,0},{6,2},{8,12},{10,14},{12,8},{14,10},{16,20},{18,... | collective-permute-start | bytes 98312 | tf_op jit(solution)/shard_map/ppermute | solution.py:18
  14.3 2.5 %collective-permute-done.2 = f32[64,128]{1,0:T(8,128)S(1)} collective-permute-done((f32[64,128]{1,0:T(8,128)S(1)}, f32[64,128]{1,0:T(8,128)S(1)}, u32[]{:S(2)}, u32[]{:S(2)}) %collective-permute-start.2) | collective-permute-done | bytes 32800 | tf_op jit(solution)/shard_map/ppermute | solution.py:18
  16.8 1.2 %collective-permute-start.3 = (f32[128,128]{1,0:T(8,128)S(1)}, f32[128,128]{1,0:T(8,128)S(1)}, u32[]{:S(2)}, u32[]{:S(2)}) collective-permute-start(f32[128,128]{1,0:T(8,128)S(1)} %pad_maximum_fusion.1), channel_id=1, source_target_pairs={{0,192},{2,194},{4,196},{6,198},{8,200},{10,202},{12,204},{14,206}... | collective-permute-start | bytes 196616 | tf_op jit(solution)/shard_map/ppermute | solution.py:18
  18.0 0.7 %multiply_add_fusion.1 = s32[2048]{0:T(1024)S(1)} fusion(s32[2048]{0:T(1024)} %param.9, s32[]{:T(128)S(6)} %add.10), kind=kLoop, calls=%fused_computation.4 | loop fusion | flops 94208 | bytes 16388 | tf_op jit(solution)/shard_map/add | solution.py:139
  18.8 0.7 %concatenate.15.labels = s32[2128]{0:T(1024)S(1)} concatenate(s32[2048]{0:T(1024)S(1)} %multiply_add_fusion.1, s32[64]{0:T(128)} %param.7, s32[16]{0:T(128)} %param.8), dimensions={0} | concatenate | bytes 17024 | tf_op jit(solution)/shard_map/concatenate | solution.py:139
  19.5 0.7 %collective-permute-done.3 = f32[128,128]{1,0:T(8,128)S(1)} collective-permute-done((f32[128,128]{1,0:T(8,128)S(1)}, f32[128,128]{1,0:T(8,128)S(1)}, u32[]{:S(2)}, u32[]{:S(2)}) %collective-permute-start.3) | collective-permute-done | bytes 65568 | tf_op jit(solution)/shard_map/ppermute | solution.py:18
  20.3 1.4 %collective-permute-start.4 = (f32[256,128]{1,0:T(8,128)S(1)}, f32[256,128]{1,0:T(8,128)S(1)}, u32[]{:S(2)}, u32[]{:S(2)}) collective-permute-start(f32[256,128]{1,0:T(8,128)S(1)} %pad_maximum_fusion.rest_0_), channel_id=1, source_target_pairs={{0,2},{2,0},{4,6},{6,4},{8,10},{10,8},{12,14},{14,12},{16,80},{18,... | collective-permute-start | bytes 393224 | tf_op jit(solution)/shard_map/ppermute | solution.py:18
  21.6 2.4 %collective-permute-start.7 = (f32[256,128]{1,0:T(8,128)S(1)}, f32[256,128]{1,0:T(8,128)S(1)}, u32[]{:S(2)}, u32[]{:S(2)}) collective-permute-start(f32[256,128]{1,0:T(8,128)S(1)} %pad_maximum_fusion.rest_0_), channel_id=1, source_target_pairs={{0,96},{2,98},{4,100},{6,102},{8,104},{10,106},{12,108},{14,110},{... | collective-permute-start | bytes 393224 | tf_op jit(solution)/shard_map/ppermute | solution.py:18
  24.0 0.8 %collective-permute-start.6 = (f32[256,128]{1,0:T(8,128)S(1)}, f32[256,128]{1,0:T(8,128)S(1)}, u32[]{:S(2)}, u32[]{:S(2)}) collective-permute-start(f32[256,128]{1,0:T(8,128)S(1)} %pad_maximum_fusion.rest_0_), channel_id=1, source_target_pairs={{0,64},{2,66},{4,68},{6,70},{8,72},{10,74},{12,76},{14,78},{16,208... | collective-permute-start | bytes 393224 | tf_op jit(solution)/shard_map/ppermute | solution.py:18
  24.8 0.7 %collective-permute-start.5 = (f32[256,128]{1,0:T(8,128)S(1)}, f32[256,128]{1,0:T(8,128)S(1)}, u32[]{:S(2)}, u32[]{:S(2)}) collective-permute-start(f32[256,128]{1,0:T(8,128)S(1)} %pad_maximum_fusion.rest_0_), channel_id=1, source_target_pairs={{0,32},{2,34},{4,36},{6,38},{8,40},{10,42},{12,44},{14,46},{16,18}... | collective-permute-start | bytes 393224 | tf_op jit(solution)/shard_map/ppermute | solution.py:18
  25.5 0.0 collective-permute-done.4.rest_1_
  25.5 1.9 %collective-permute-start.10 = (f32[256,128]{1,0:T(8,128)S(1)}, f32[256,128]{1,0:T(8,128)S(1)}, u32[]{:S(2)}, u32[]{:S(2)}) collective-permute-start(f32[256,128]{1,0:T(8,128)S(1)} %collective-permute-done.4.rest_1_), channel_id=1, source_target_pairs={{0,64},{2,66},{4,68},{6,70},{8,72},{10,74},{12,76},{14,78},{16,208... | collective-permute-start | bytes 393224 | tf_op jit(solution)/shard_map/ppermute | solution.py:18
  27.4 1.2 %collective-permute-start.8 = (f32[256,128]{1,0:T(8,128)S(1)}, f32[256,128]{1,0:T(8,128)S(1)}, u32[]{:S(2)}, u32[]{:S(2)}) collective-permute-start(f32[256,128]{1,0:T(8,128)S(1)} %collective-permute-done.4.rest_1_), channel_id=1, source_target_pairs={{0,96},{2,98},{4,100},{6,102},{8,104},{10,106},{12,108},{14,110},{... | collective-permute-start | bytes 393224 | tf_op jit(solution)/shard_map/ppermute | solution.py:18
  28.6 0.0 collective-permute-done.7.rest_6_
  28.6 5.7 %collective-permute-start.11 = (f32[256,128]{1,0:T(8,128)S(1)}, f32[256,128]{1,0:T(8,128)S(1)}, u32[]{:S(2)}, u32[]{:S(2)}) collective-permute-start(f32[256,128]{1,0:T(8,128)S(1)} %pad_maximum_fusion.rest_0_), channel_id=1, source_target_pairs={{0,16},{2,18},{4,20},{6,22},{8,24},{10,26},{12,28},{14,30},{16,0},... | collective-permute-start | bytes 393224 | tf_op jit(solution)/shard_map/ppermute | solution.py:18
  34.4 0.0 collective-permute-done.6.rest_4_
  34.4 0.7 %collective-permute-start.9 = (f32[256,128]{1,0:T(8,128)S(1)}, f32[256,128]{1,0:T(8,128)S(1)}, u32[]{:S(2)}, u32[]{:S(2)}) collective-permute-start(f32[256,128]{1,0:T(8,128)S(1)} %collective-permute-done.4.rest_1_), channel_id=1, source_target_pairs={{0,32},{2,34},{4,36},{6,38},{8,40},{10,42},{12,44},{14,46},{16,18}... | collective-permute-start | bytes 393224 | tf_op jit(solution)/shard_map/ppermute | solution.py:18
  35.1 0.0 collective-permute-done.5.rest_2_
  35.1 0.9 %collective-permute-start.12 = (f32[256,128]{1,0:T(8,128)S(1)}, f32[256,128]{1,0:T(8,128)S(1)}, u32[]{:S(2)}, u32[]{:S(2)}) collective-permute-start(f32[256,128]{1,0:T(8,128)S(1)} %collective-permute-done.4.rest_1_), channel_id=1, source_target_pairs={{0,16},{2,18},{4,20},{6,22},{8,24},{10,26},{12,28},{14,30},{16,0},... | collective-permute-start | bytes 393224 | tf_op jit(solution)/shard_map/ppermute | solution.py:18
  36.0 0.0 collective-permute-done.10.rest_5_
  36.0 0.3 collective-permute-start.16
  36.4 0.0 collective-permute-done.8.rest_7_
  36.4 2.7 %collective-permute-start.13 = (f32[256,128]{1,0:T(8,128)S(1)}, f32[256,128]{1,0:T(8,128)S(1)}, u32[]{:S(2)}, u32[]{:S(2)}) collective-permute-start(f32[256,128]{1,0:T(8,128)S(1)} %collective-permute-done.5.rest_2_), channel_id=1, source_target_pairs={{0,16},{2,18},{4,20},{6,22},{8,24},{10,26},{12,28},{14,30},{16,0},... | collective-permute-start | bytes 393224 | tf_op jit(solution)/shard_map/ppermute | solution.py:18
  39.0 0.0 collective-permute-done.11.rest_8_
  39.1 0.0 collective-permute-start.15
  39.1 0.0 collective-permute-done.9.rest_3_
  39.1 0.9 %collective-permute-start.14 = (f32[256,128]{1,0:T(8,128)S(1)}, f32[256,128]{1,0:T(8,128)S(1)}, u32[]{:S(2)}, u32[]{:S(2)}) collective-permute-start(f32[256,128]{1,0:T(8,128)S(1)} %collective-permute-done.9.rest_3_), channel_id=1, source_target_pairs={{0,16},{2,18},{4,20},{6,22},{8,24},{10,26},{12,28},{14,30},{16,0},... | collective-permute-start | bytes 393224 | tf_op jit(solution)/shard_map/ppermute | solution.py:18
  40.0 0.0 collective-permute-done.12.rest_9_
  40.0 0.0 collective-permute-start.17
  40.0 0.0 collective-permute-done.16.rest_13_
  40.0 0.5 %collective-permute-start.18 = (f32[256,128]{1,0:T(8,128)S(1)}, f32[256,128]{1,0:T(8,128)S(1)}, u32[]{:S(2)}, u32[]{:S(2)}) collective-permute-start(f32[256,128]{1,0:T(8,128)S(1)} %collective-permute-done.8.rest_7_), channel_id=1, source_target_pairs={{0,16},{2,18},{4,20},{6,22},{8,24},{10,26},{12,28},{14,30},{16,0},... | collective-permute-start | bytes 393224 | tf_op jit(solution)/shard_map/ppermute | solution.py:18
  40.5 0.5 collective-permute-done.14.rest_11_
  40.9 0.0 collective-permute-done.13.rest_10_
  40.9 0.0 collective-permute-done.15.rest_12_
  40.9 0.4 collective-permute-done.17.rest_14_
  41.3 0.2 collective-permute-done.18.rest_15_
  41.5 8.1 %shard_map.55 = f32[8192,256]{1,0:T(8,128)} custom-call(s32[2128]{0:T(1024)S(1)} %concatenate.15.labels, f32[8192,256]{1,0:T(8,128)} %integrals.1, f32[256,128]{1,0:T(8,128)S(1)} %pad_maximum_fusion.rest_0_, f32[256,128]{1,0:T(8,128)S(1)} %collective-permute-done.4.rest_1_, f32[256,128]{1,0:T(8,128)S(1)} %collective-permute-done.5.rest_2_, ...), custom_call_target="tpu_custom_call" | custom-call | tf_op jit(solution)/shard_map/pallas_call | solution.py:111
  (4 shorter events, 0.0 us)
Async XLA Ops:
  0.0 4.9 %collective-permute-start = (f32[16,256]{1,0:T(8,128)}, f32[16,256]{1,0:T(8,128)S(1)}, u32[]{:S(2)}, u32[]{:S(2)}) collective-permute-start(f32[16,256]{1,0:T(8,128)} %param.6), channel_id=1, source_target_pairs={{0,1},{1,0},{2,3},{3,2},{4,5},{5,4},{6,7},{7,6},{8,9},{9,8},{10,11... | collective-permute-start | bytes 49160 | tf_op jit(solution)/shard_map/ppermute | solution.py:23
  5.8 7.4 %collective-permute-start.1 = (f32[32,128]{1,0:T(8,128)S(1)}, f32[32,128]{1,0:T(8,128)S(1)}, u32[]{:S(2)}, u32[]{:S(2)}) collective-permute-start(f32[32,128]{1,0:T(8,128)S(1)} %reshape.3), channel_id=1, source_target_pairs={{0,12},{2,14},{4,8},{6,10},{8,4},{10,6},{12,0},{14,2},{16,28},{18,... | collective-permute-start | bytes 49160 | tf_op jit(solution)/shard_map/ppermute | solution.py:18
  13.2 3.7 %collective-permute-start.2 = (f32[64,128]{1,0:T(8,128)S(1)}, f32[64,128]{1,0:T(8,128)S(1)}, u32[]{:S(2)}, u32[]{:S(2)}) collective-permute-start(f32[64,128]{1,0:T(8,128)S(1)} %pad_maximum_fusion.2), channel_id=1, source_target_pairs={{0,4},{2,6},{4,0},{6,2},{8,12},{10,14},{12,8},{14,10},{16,20},{18,... | collective-permute-start | bytes 98312 | tf_op jit(solution)/shard_map/ppermute | solution.py:18
  16.8 3.4 %collective-permute-start.3 = (f32[128,128]{1,0:T(8,128)S(1)}, f32[128,128]{1,0:T(8,128)S(1)}, u32[]{:S(2)}, u32[]{:S(2)}) collective-permute-start(f32[128,128]{1,0:T(8,128)S(1)} %pad_maximum_fusion.1), channel_id=1, source_target_pairs={{0,192},{2,194},{4,196},{6,198},{8,200},{10,202},{12,204},{14,206}... | collective-permute-start | bytes 196616 | tf_op jit(solution)/shard_map/ppermute | solution.py:18
  20.3 5.2 %collective-permute-start.4 = (f32[256,128]{1,0:T(8,128)S(1)}, f32[256,128]{1,0:T(8,128)S(1)}, u32[]{:S(2)}, u32[]{:S(2)}) collective-permute-start(f32[256,128]{1,0:T(8,128)S(1)} %pad_maximum_fusion.rest_0_), channel_id=1, source_target_pairs={{0,2},{2,0},{4,6},{6,4},{8,10},{10,8},{12,14},{14,12},{16,80},{18,... | collective-permute-start | bytes 393224 | tf_op jit(solution)/shard_map/ppermute | solution.py:18
  21.6 7.0 %collective-permute-start.7 = (f32[256,128]{1,0:T(8,128)S(1)}, f32[256,128]{1,0:T(8,128)S(1)}, u32[]{:S(2)}, u32[]{:S(2)}) collective-permute-start(f32[256,128]{1,0:T(8,128)S(1)} %pad_maximum_fusion.rest_0_), channel_id=1, source_target_pairs={{0,96},{2,98},{4,100},{6,102},{8,104},{10,106},{12,108},{14,110},{... | collective-permute-start | bytes 393224 | tf_op jit(solution)/shard_map/ppermute | solution.py:18
  24.0 10.4 %collective-permute-start.6 = (f32[256,128]{1,0:T(8,128)S(1)}, f32[256,128]{1,0:T(8,128)S(1)}, u32[]{:S(2)}, u32[]{:S(2)}) collective-permute-start(f32[256,128]{1,0:T(8,128)S(1)} %pad_maximum_fusion.rest_0_), channel_id=1, source_target_pairs={{0,64},{2,66},{4,68},{6,70},{8,72},{10,74},{12,76},{14,78},{16,208... | collective-permute-start | bytes 393224 | tf_op jit(solution)/shard_map/ppermute | solution.py:18
  24.8 10.3 %collective-permute-start.5 = (f32[256,128]{1,0:T(8,128)S(1)}, f32[256,128]{1,0:T(8,128)S(1)}, u32[]{:S(2)}, u32[]{:S(2)}) collective-permute-start(f32[256,128]{1,0:T(8,128)S(1)} %pad_maximum_fusion.rest_0_), channel_id=1, source_target_pairs={{0,32},{2,34},{4,36},{6,38},{8,40},{10,42},{12,44},{14,46},{16,18}... | collective-permute-start | bytes 393224 | tf_op jit(solution)/shard_map/ppermute | solution.py:18
  25.5 10.5 %collective-permute-start.10 = (f32[256,128]{1,0:T(8,128)S(1)}, f32[256,128]{1,0:T(8,128)S(1)}, u32[]{:S(2)}, u32[]{:S(2)}) collective-permute-start(f32[256,128]{1,0:T(8,128)S(1)} %collective-permute-done.4.rest_1_), channel_id=1, source_target_pairs={{0,64},{2,66},{4,68},{6,70},{8,72},{10,74},{12,76},{14,78},{16,208... | collective-permute-start | bytes 393224 | tf_op jit(solution)/shard_map/ppermute | solution.py:18
  27.4 9.0 %collective-permute-start.8 = (f32[256,128]{1,0:T(8,128)S(1)}, f32[256,128]{1,0:T(8,128)S(1)}, u32[]{:S(2)}, u32[]{:S(2)}) collective-permute-start(f32[256,128]{1,0:T(8,128)S(1)} %collective-permute-done.4.rest_1_), channel_id=1, source_target_pairs={{0,96},{2,98},{4,100},{6,102},{8,104},{10,106},{12,108},{14,110},{... | collective-permute-start | bytes 393224 | tf_op jit(solution)/shard_map/ppermute | solution.py:18
  28.6 10.4 %collective-permute-start.11 = (f32[256,128]{1,0:T(8,128)S(1)}, f32[256,128]{1,0:T(8,128)S(1)}, u32[]{:S(2)}, u32[]{:S(2)}) collective-permute-start(f32[256,128]{1,0:T(8,128)S(1)} %pad_maximum_fusion.rest_0_), channel_id=1, source_target_pairs={{0,16},{2,18},{4,20},{6,22},{8,24},{10,26},{12,28},{14,30},{16,0},... | collective-permute-start | bytes 393224 | tf_op jit(solution)/shard_map/ppermute | solution.py:18
  34.4 4.7 %collective-permute-start.9 = (f32[256,128]{1,0:T(8,128)S(1)}, f32[256,128]{1,0:T(8,128)S(1)}, u32[]{:S(2)}, u32[]{:S(2)}) collective-permute-start(f32[256,128]{1,0:T(8,128)S(1)} %collective-permute-done.4.rest_1_), channel_id=1, source_target_pairs={{0,32},{2,34},{4,36},{6,38},{8,40},{10,42},{12,44},{14,46},{16,18}... | collective-permute-start | bytes 393224 | tf_op jit(solution)/shard_map/ppermute | solution.py:18
  35.1 4.8 %collective-permute-start.12 = (f32[256,128]{1,0:T(8,128)S(1)}, f32[256,128]{1,0:T(8,128)S(1)}, u32[]{:S(2)}, u32[]{:S(2)}) collective-permute-start(f32[256,128]{1,0:T(8,128)S(1)} %collective-permute-done.4.rest_1_), channel_id=1, source_target_pairs={{0,16},{2,18},{4,20},{6,22},{8,24},{10,26},{12,28},{14,30},{16,0},... | collective-permute-start | bytes 393224 | tf_op jit(solution)/shard_map/ppermute | solution.py:18
  36.0 3.9 %collective-permute-start.16 = (f32[256,128]{1,0:T(8,128)S(1)}, f32[256,128]{1,0:T(8,128)S(1)}, u32[]{:S(2)}, u32[]{:S(2)}) collective-permute-start(f32[256,128]{1,0:T(8,128)S(1)} %collective-permute-done.10.rest_5_), channel_id=1, source_target_pairs={{0,16},{2,18},{4,20},{6,22},{8,24},{10,26},{12,28},{14,30},{16,0},... | collective-permute-start | bytes 393224 | tf_op jit(solution)/shard_map/ppermute | solution.py:18
  36.4 4.6 %collective-permute-start.13 = (f32[256,128]{1,0:T(8,128)S(1)}, f32[256,128]{1,0:T(8,128)S(1)}, u32[]{:S(2)}, u32[]{:S(2)}) collective-permute-start(f32[256,128]{1,0:T(8,128)S(1)} %collective-permute-done.5.rest_2_), channel_id=1, source_target_pairs={{0,16},{2,18},{4,20},{6,22},{8,24},{10,26},{12,28},{14,30},{16,0},... | collective-permute-start | bytes 393224 | tf_op jit(solution)/shard_map/ppermute | solution.py:18
  39.1 1.9 %collective-permute-start.15 = (f32[256,128]{1,0:T(8,128)S(1)}, f32[256,128]{1,0:T(8,128)S(1)}, u32[]{:S(2)}, u32[]{:S(2)}) collective-permute-start(f32[256,128]{1,0:T(8,128)S(1)} %collective-permute-done.6.rest_4_), channel_id=1, source_target_pairs={{0,16},{2,18},{4,20},{6,22},{8,24},{10,26},{12,28},{14,30},{16,0},... | collective-permute-start | bytes 393224 | tf_op jit(solution)/shard_map/ppermute | solution.py:18
  39.1 1.9 %collective-permute-start.14 = (f32[256,128]{1,0:T(8,128)S(1)}, f32[256,128]{1,0:T(8,128)S(1)}, u32[]{:S(2)}, u32[]{:S(2)}) collective-permute-start(f32[256,128]{1,0:T(8,128)S(1)} %collective-permute-done.9.rest_3_), channel_id=1, source_target_pairs={{0,16},{2,18},{4,20},{6,22},{8,24},{10,26},{12,28},{14,30},{16,0},... | collective-permute-start | bytes 393224 | tf_op jit(solution)/shard_map/ppermute | solution.py:18
  40.0 1.3 %collective-permute-start.17 = (f32[256,128]{1,0:T(8,128)S(1)}, f32[256,128]{1,0:T(8,128)S(1)}, u32[]{:S(2)}, u32[]{:S(2)}) collective-permute-start(f32[256,128]{1,0:T(8,128)S(1)} %collective-permute-done.7.rest_6_), channel_id=1, source_target_pairs={{0,16},{2,18},{4,20},{6,22},{8,24},{10,26},{12,28},{14,30},{16,0},... | collective-permute-start | bytes 393224 | tf_op jit(solution)/shard_map/ppermute | solution.py:18
  40.0 1.5 %collective-permute-start.18 = (f32[256,128]{1,0:T(8,128)S(1)}, f32[256,128]{1,0:T(8,128)S(1)}, u32[]{:S(2)}, u32[]{:S(2)}) collective-permute-start(f32[256,128]{1,0:T(8,128)S(1)} %collective-permute-done.8.rest_7_), channel_id=1, source_target_pairs={{0,16},{2,18},{4,20},{6,22},{8,24},{10,26},{12,28},{14,30},{16,0},... | collective-permute-start | bytes 393224 | tf_op jit(solution)/shard_map/ppermute | solution.py:18

commit v5 on v4

--- a/solution.py
+++ b/solution.py
@@ -10,7 +10,7 @@
 STEPS = ((Z6, Z6), (Z2, Z2), (Y3, X1), (Z1, Y1), (X1, Z1), (Y1, Y3))
 
 CHUNK = 512
-STRIDE = 2048
+STRIDE = 4096
 
 
 def trade(block, masks):
@@ -140,10 +140,10 @@
 
     parity = (1 - 2 * lax.axis_index("ao")).astype(jnp.float32)
     partner = trade_raw(amplitudes, (1, 1))
-    block = (partner[:, ::-1] + parity * amplitudes).reshape(-1, 128)
+    partner, scaled, labels = lax.optimization_barrier((partner, parity * amplitudes, labels))
+    block = (partner[:, ::-1] + scaled).reshape(-1, 128)
     for masks in STEPS[:-3]:
         block = lax.optimization_barrier(jnp.concatenate([block, trade(block, masks)]))
-    block, labels = lax.optimization_barrier((block, labels))
     a, b = STEPS[-2:]
     both = tuple(p ^ q for p, q in zip(a, b))
     later = trade(block, STEPS[-3])

time: 50.1 us -> 49 us (0.978)
  starting transfers between devices: 32.4 us -> 31.2 us
  waiting for transfers between devices: 6.73 us -> 7.24 us
    ppermute x18, waiting for transfers between devices: 5.4 us -> 7.23 us  [trade(): lax.ppermute(block, ('aa', 'ba'), [(i, j) for i, j in route if i != j])]
    ppermute x1, waiting for transfers between devices: 1.34 us -> 0.01 us  [trade_raw(): lax.ppermute(amplitudes, ('aa', 'ba', 'ao'), [(i, j) for i, j in route if...]
    ppermute x18, starting transfers between devices: 28.8 us -> 27.6 us  [trade(): lax.ppermute(block, ('aa', 'ba'), [(i, j) for i, j in route if i != j])]
    mul x0 -> x1, other arithmetic: none -> 0.75 us  [on_device(): parity * amplitudes]
    add x1, other arithmetic: 0.73 us -> 0.01 us  [on_device(): block = (partner[:, ::-1] + scaled).reshape(-1, 128)]
  transfers between devices with their start and end apart: 19 -> 19, of which waited for: 7 -> 6; matrix products, arithmetic and copies ran while one was open for 3% -> 5% of each run, Pallas kernels for 0% -> 0%
where the time goes in v5:
time: 49 us; the launch traced here: 48.6 us
  starting transfers between devices  31.2 us (64%)
  Pallas kernels  7.7 us (16%)
  waiting for transfers between devices  7.24 us (15%)
  other arithmetic  1.49 us (3%)
  local copies, waits for them, and re-layouts  0.9 us (2%)
    ppermute x18, starting transfers between devices, trade(): lax.ppermute(block, ('aa', 'ba'), [(i, j) for i, j in route if i != j])  27.6 us
    pallas_call x1, Pallas kernels, ladder(): pl.pallas_call(ladder_kernel, out_shape=jax.ShapeDtypeStruct((rows, 256),...  7.7 us
    ppermute x18, waiting for transfers between devices, trade(): lax.ppermute(block, ('aa', 'ba'), [(i, j) for i, j in route if i != j])  7.23 us
    ppermute x1, starting transfers between devices, trade_raw(): lax.ppermute(amplitudes, ('aa', 'ba', 'ao'), [(i, j) for i, j in route if...  3.57 us
  transfers between devices with their start and end apart: 19, of which 6 were waited for; matrix products, arithmetic and copies ran while one was open for 5% of the time, Pallas kernels for 0%

profile of v5, /device:TPU:1, one launch (start us, length us, event | category | flops | bytes accessed | tf_op | source)
XLA Modules:
  0.0 48.6 jit_solution(6953337090356088607)
XLA Ops:
  0.0 3.6 %collective-permute-start = (f32[16,256]{1,0:T(8,128)}, f32[16,256]{1,0:T(8,128)S(1)}, u32[]{:S(2)}, u32[]{:S(2)}) collective-permute-start(f32[16,256]{1,0:T(8,128)} %param.6), channel_id=1, source_target_pairs={{0,1},{1,0},{2,3},{3,2},{4,5},{5,4},{6,7},{7,6},{8,9},{9,8},{10,11... | collective-permute-start | bytes 49160 | tf_op jit(solution)/shard_map/ppermute | solution.py:23
  3.6 0.8 %broadcast_multiply_fusion = f32[16,256]{1,0:T(8,128)S(1)} fusion(f32[16,256]{1,0:T(8,128)} %param.6, f32[]{:T(128)S(6)} %convert_element_type.3), kind=kLoop, calls=%fused_computation.11 | loop fusion | flops 4096 | bytes 32772 | tf_op jit(solution)/shard_map/mul | solution.py:143
  4.3 0.7 %multiply_add_fusion = s32[2048]{0:T(1024)S(1)} fusion(s32[2048]{0:T(1024)} %param.9, s32[]{:T(128)S(6)} %add.9), kind=kLoop, calls=%fused_computation.3 | loop fusion | flops 94208 | bytes 16388 | tf_op jit(solution)/shard_map/add | solution.py:139
  5.0 0.7 %concatenate.12.labels = s32[2128]{0:T(1024)S(1)} concatenate(s32[2048]{0:T(1024)S(1)} %multiply_add_fusion, s32[64]{0:T(128)} %param.7, s32[16]{0:T(128)} %param.8), dimensions={0} | concatenate | bytes 17024 | tf_op jit(solution)/shard_map/concatenate | solution.py:139
  5.8 0.0 collective-permute-done
  5.8 0.1 rev.3
  6.0 6.1 %collective-permute-start.1 = (f32[32,128]{1,0:T(8,128)S(1)}, f32[32,128]{1,0:T(8,128)S(1)}, u32[]{:S(2)}, u32[]{:S(2)}) collective-permute-start(f32[32,128]{1,0:T(8,128)S(1)} %reshape.3), channel_id=1, source_target_pairs={{0,12},{2,14},{4,8},{6,10},{8,4},{10,6},{12,0},{14,2},{16,28},{18,... | collective-permute-start | bytes 49160 | tf_op jit(solution)/shard_map/ppermute | solution.py:18
  12.1 1.1 %collective-permute-done.1 = f32[32,128]{1,0:T(8,128)S(1)} collective-permute-done((f32[32,128]{1,0:T(8,128)S(1)}, f32[32,128]{1,0:T(8,128)S(1)}, u32[]{:S(2)}, u32[]{:S(2)}) %collective-permute-start.1) | collective-permute-done | bytes 16416 | tf_op jit(solution)/shard_map/ppermute | solution.py:18
  13.2 1.2 %collective-permute-start.2 = (f32[64,128]{1,0:T(8,128)S(1)}, f32[64,128]{1,0:T(8,128)S(1)}, u32[]{:S(2)}, u32[]{:S(2)}) collective-permute-start(f32[64,128]{1,0:T(8,128)S(1)} %pad_maximum_fusion.2), channel_id=1, source_target_pairs={{0,4},{2,6},{4,0},{6,2},{8,12},{10,14},{12,8},{14,10},{16,20},{18,... | collective-permute-start | bytes 98312 | tf_op jit(solution)/shard_map/ppermute | solution.py:18
  14.4 2.5 %collective-permute-done.2 = f32[64,128]{1,0:T(8,128)S(1)} collective-permute-done((f32[64,128]{1,0:T(8,128)S(1)}, f32[64,128]{1,0:T(8,128)S(1)}, u32[]{:S(2)}, u32[]{:S(2)}) %collective-permute-start.2) | collective-permute-done | bytes 32800 | tf_op jit(solution)/shard_map/ppermute | solution.py:18
  16.9 0.5 %collective-permute-start.3 = (f32[128,128]{1,0:T(8,128)S(1)}, f32[128,128]{1,0:T(8,128)S(1)}, u32[]{:S(2)}, u32[]{:S(2)}) collective-permute-start(f32[128,128]{1,0:T(8,128)S(1)} %pad_maximum_fusion.1), channel_id=1, source_target_pairs={{0,192},{2,194},{4,196},{6,198},{8,200},{10,202},{12,204},{14,206}... | collective-permute-start | bytes 196616 | tf_op jit(solution)/shard_map/ppermute | solution.py:18
  17.4 2.6 %collective-permute-done.3 = f32[128,128]{1,0:T(8,128)S(1)} collective-permute-done((f32[128,128]{1,0:T(8,128)S(1)}, f32[128,128]{1,0:T(8,128)S(1)}, u32[]{:S(2)}, u32[]{:S(2)}) %collective-permute-start.3) | collective-permute-done | bytes 65568 | tf_op jit(solution)/shard_map/ppermute | solution.py:18
  20.0 1.4 %collective-permute-start.4 = (f32[256,128]{1,0:T(8,128)S(1)}, f32[256,128]{1,0:T(8,128)S(1)}, u32[]{:S(2)}, u32[]{:S(2)}) collective-permute-start(f32[256,128]{1,0:T(8,128)S(1)} %pad_maximum_fusion.rest_0_), channel_id=1, source_target_pairs={{0,2},{2,0},{4,6},{6,4},{8,10},{10,8},{12,14},{14,12},{16,80},{18,... | collective-permute-start | bytes 393224 | tf_op jit(solution)/shard_map/ppermute | solution.py:18
  21.4 2.4 %collective-permute-start.7 = (f32[256,128]{1,0:T(8,128)S(1)}, f32[256,128]{1,0:T(8,128)S(1)}, u32[]{:S(2)}, u32[]{:S(2)}) collective-permute-start(f32[256,128]{1,0:T(8,128)S(1)} %pad_maximum_fusion.rest_0_), channel_id=1, source_target_pairs={{0,96},{2,98},{4,100},{6,102},{8,104},{10,106},{12,108},{14,110},{... | collective-permute-start | bytes 393224 | tf_op jit(solution)/shard_map/ppermute | solution.py:18
  23.7 0.8 %collective-permute-start.6 = (f32[256,128]{1,0:T(8,128)S(1)}, f32[256,128]{1,0:T(8,128)S(1)}, u32[]{:S(2)}, u32[]{:S(2)}) collective-permute-start(f32[256,128]{1,0:T(8,128)S(1)} %pad_maximum_fusion.rest_0_), channel_id=1, source_target_pairs={{0,64},{2,66},{4,68},{6,70},{8,72},{10,74},{12,76},{14,78},{16,208... | collective-permute-start | bytes 393224 | tf_op jit(solution)/shard_map/ppermute | solution.py:18
  24.5 0.7 %collective-permute-start.5 = (f32[256,128]{1,0:T(8,128)S(1)}, f32[256,128]{1,0:T(8,128)S(1)}, u32[]{:S(2)}, u32[]{:S(2)}) collective-permute-start(f32[256,128]{1,0:T(8,128)S(1)} %pad_maximum_fusion.rest_0_), channel_id=1, source_target_pairs={{0,32},{2,34},{4,36},{6,38},{8,40},{10,42},{12,44},{14,46},{16,18}... | collective-permute-start | bytes 393224 | tf_op jit(solution)/shard_map/ppermute | solution.py:18
  25.2 0.0 collective-permute-done.4.rest_1_
  25.2 1.9 %collective-permute-start.10 = (f32[256,128]{1,0:T(8,128)S(1)}, f32[256,128]{1,0:T(8,128)S(1)}, u32[]{:S(2)}, u32[]{:S(2)}) collective-permute-start(f32[256,128]{1,0:T(8,128)S(1)} %collective-permute-done.4.rest_1_), channel_id=1, source_target_pairs={{0,64},{2,66},{4,68},{6,70},{8,72},{10,74},{12,76},{14,78},{16,208... | collective-permute-start | bytes 393224 | tf_op jit(solution)/shard_map/ppermute | solution.py:18
  27.1 1.2 %collective-permute-start.8 = (f32[256,128]{1,0:T(8,128)S(1)}, f32[256,128]{1,0:T(8,128)S(1)}, u32[]{:S(2)}, u32[]{:S(2)}) collective-permute-start(f32[256,128]{1,0:T(8,128)S(1)} %collective-permute-done.4.rest_1_), channel_id=1, source_target_pairs={{0,96},{2,98},{4,100},{6,102},{8,104},{10,106},{12,108},{14,110},{... | collective-permute-start | bytes 393224 | tf_op jit(solution)/shard_map/ppermute | solution.py:18
  28.4 0.0 collective-permute-done.7.rest_6_
  28.4 5.4 %collective-permute-start.11 = (f32[256,128]{1,0:T(8,128)S(1)}, f32[256,128]{1,0:T(8,128)S(1)}, u32[]{:S(2)}, u32[]{:S(2)}) collective-permute-start(f32[256,128]{1,0:T(8,128)S(1)} %pad_maximum_fusion.rest_0_), channel_id=1, source_target_pairs={{0,16},{2,18},{4,20},{6,22},{8,24},{10,26},{12,28},{14,30},{16,0},... | collective-permute-start | bytes 393224 | tf_op jit(solution)/shard_map/ppermute | solution.py:18
  33.7 0.0 collective-permute-done.6.rest_4_
  33.7 0.7 %collective-permute-start.9 = (f32[256,128]{1,0:T(8,128)S(1)}, f32[256,128]{1,0:T(8,128)S(1)}, u32[]{:S(2)}, u32[]{:S(2)}) collective-permute-start(f32[256,128]{1,0:T(8,128)S(1)} %collective-permute-done.4.rest_1_), channel_id=1, source_target_pairs={{0,32},{2,34},{4,36},{6,38},{8,40},{10,42},{12,44},{14,46},{16,18}... | collective-permute-start | bytes 393224 | tf_op jit(solution)/shard_map/ppermute | solution.py:18
  34.5 0.0 collective-permute-done.5.rest_2_
  34.5 0.4 collective-permute-start.12
  34.8 0.0 collective-permute-done.10.rest_5_
  34.8 0.9 %collective-permute-start.16 = (f32[256,128]{1,0:T(8,128)S(1)}, f32[256,128]{1,0:T(8,128)S(1)}, u32[]{:S(2)}, u32[]{:S(2)}) collective-permute-start(f32[256,128]{1,0:T(8,128)S(1)} %collective-permute-done.10.rest_5_), channel_id=1, source_target_pairs={{0,16},{2,18},{4,20},{6,22},{8,24},{10,26},{12,28},{14,30},{16,0},... | collective-permute-start | bytes 393224 | tf_op jit(solution)/shard_map/ppermute | solution.py:18
  35.8 0.0 collective-permute-done.8.rest_7_
  35.8 2.4 %collective-permute-start.13 = (f32[256,128]{1,0:T(8,128)S(1)}, f32[256,128]{1,0:T(8,128)S(1)}, u32[]{:S(2)}, u32[]{:S(2)}) collective-permute-start(f32[256,128]{1,0:T(8,128)S(1)} %collective-permute-done.5.rest_2_), channel_id=1, source_target_pairs={{0,16},{2,18},{4,20},{6,22},{8,24},{10,26},{12,28},{14,30},{16,0},... | collective-permute-start | bytes 393224 | tf_op jit(solution)/shard_map/ppermute | solution.py:18
  38.2 0.0 collective-permute-done.11.rest_8_
  38.2 0.0 collective-permute-start.15
  38.2 0.0 collective-permute-done.9.rest_3_
  38.2 1.1 %collective-permute-start.14 = (f32[256,128]{1,0:T(8,128)S(1)}, f32[256,128]{1,0:T(8,128)S(1)}, u32[]{:S(2)}, u32[]{:S(2)}) collective-permute-start(f32[256,128]{1,0:T(8,128)S(1)} %collective-permute-done.9.rest_3_), channel_id=1, source_target_pairs={{0,16},{2,18},{4,20},{6,22},{8,24},{10,26},{12,28},{14,30},{16,0},... | collective-permute-start | bytes 393224 | tf_op jit(solution)/shard_map/ppermute | solution.py:18
  39.3 0.0 collective-permute-done.12.rest_9_
  39.3 0.0 collective-permute-start.17
  39.3 0.0 collective-permute-done.16.rest_13_
  39.3 0.5 %collective-permute-start.18 = (f32[256,128]{1,0:T(8,128)S(1)}, f32[256,128]{1,0:T(8,128)S(1)}, u32[]{:S(2)}, u32[]{:S(2)}) collective-permute-start(f32[256,128]{1,0:T(8,128)S(1)} %collective-permute-done.8.rest_7_), channel_id=1, source_target_pairs={{0,16},{2,18},{4,20},{6,22},{8,24},{10,26},{12,28},{14,30},{16,0},... | collective-permute-start | bytes 393224 | tf_op jit(solution)/shard_map/ppermute | solution.py:18
  39.8 0.5 collective-permute-done.14.rest_11_
  40.3 0.0 collective-permute-done.13.rest_10_
  40.3 0.0 collective-permute-done.15.rest_12_
  40.3 0.4 collective-permute-done.17.rest_14_
  40.7 0.2 collective-permute-done.18.rest_15_
  40.9 7.7 %shard_map.55 = f32[8192,256]{1,0:T(8,128)} custom-call(s32[2128]{0:T(1024)S(1)} %concatenate.12.labels, f32[8192,256]{1,0:T(8,128)} %integrals.1, f32[256,128]{1,0:T(8,128)S(1)} %pad_maximum_fusion.rest_0_, f32[256,128]{1,0:T(8,128)S(1)} %collective-permute-done.4.rest_1_, f32[256,128]{1,0:T(8,128)S(1)} %collective-permute-done.5.rest_2_, ...), custom_call_target="tpu_custom_call" | custom-call | tf_op jit(solution)/shard_map/pallas_call | solution.py:111
  (5 shorter events, 0.0 us)
Async XLA Ops:
  0.0 5.8 %collective-permute-start = (f32[16,256]{1,0:T(8,128)}, f32[16,256]{1,0:T(8,128)S(1)}, u32[]{:S(2)}, u32[]{:S(2)}) collective-permute-start(f32[16,256]{1,0:T(8,128)} %param.6), channel_id=1, source_target_pairs={{0,1},{1,0},{2,3},{3,2},{4,5},{5,4},{6,7},{7,6},{8,9},{9,8},{10,11... | collective-permute-start | bytes 49160 | tf_op jit(solution)/shard_map/ppermute | solution.py:23
  6.0 7.2 %collective-permute-start.1 = (f32[32,128]{1,0:T(8,128)S(1)}, f32[32,128]{1,0:T(8,128)S(1)}, u32[]{:S(2)}, u32[]{:S(2)}) collective-permute-start(f32[32,128]{1,0:T(8,128)S(1)} %reshape.3), channel_id=1, source_target_pairs={{0,12},{2,14},{4,8},{6,10},{8,4},{10,6},{12,0},{14,2},{16,28},{18,... | collective-permute-start | bytes 49160 | tf_op jit(solution)/shard_map/ppermute | solution.py:18
  13.2 3.7 %collective-permute-start.2 = (f32[64,128]{1,0:T(8,128)S(1)}, f32[64,128]{1,0:T(8,128)S(1)}, u32[]{:S(2)}, u32[]{:S(2)}) collective-permute-start(f32[64,128]{1,0:T(8,128)S(1)} %pad_maximum_fusion.2), channel_id=1, source_target_pairs={{0,4},{2,6},{4,0},{6,2},{8,12},{10,14},{12,8},{14,10},{16,20},{18,... | collective-permute-start | bytes 98312 | tf_op jit(solution)/shard_map/ppermute | solution.py:18
  16.9 3.1 %collective-permute-start.3 = (f32[128,128]{1,0:T(8,128)S(1)}, f32[128,128]{1,0:T(8,128)S(1)}, u32[]{:S(2)}, u32[]{:S(2)}) collective-permute-start(f32[128,128]{1,0:T(8,128)S(1)} %pad_maximum_fusion.1), channel_id=1, source_target_pairs={{0,192},{2,194},{4,196},{6,198},{8,200},{10,202},{12,204},{14,206}... | collective-permute-start | bytes 196616 | tf_op jit(solution)/shard_map/ppermute | solution.py:18
  20.0 5.2 %collective-permute-start.4 = (f32[256,128]{1,0:T(8,128)S(1)}, f32[256,128]{1,0:T(8,128)S(1)}, u32[]{:S(2)}, u32[]{:S(2)}) collective-permute-start(f32[256,128]{1,0:T(8,128)S(1)} %pad_maximum_fusion.rest_0_), channel_id=1, source_target_pairs={{0,2},{2,0},{4,6},{6,4},{8,10},{10,8},{12,14},{14,12},{16,80},{18,... | collective-permute-start | bytes 393224 | tf_op jit(solution)/shard_map/ppermute | solution.py:18
  21.4 7.0 %collective-permute-start.7 = (f32[256,128]{1,0:T(8,128)S(1)}, f32[256,128]{1,0:T(8,128)S(1)}, u32[]{:S(2)}, u32[]{:S(2)}) collective-permute-start(f32[256,128]{1,0:T(8,128)S(1)} %pad_maximum_fusion.rest_0_), channel_id=1, source_target_pairs={{0,96},{2,98},{4,100},{6,102},{8,104},{10,106},{12,108},{14,110},{... | collective-permute-start | bytes 393224 | tf_op jit(solution)/shard_map/ppermute | solution.py:18
  23.7 10.0 %collective-permute-start.6 = (f32[256,128]{1,0:T(8,128)S(1)}, f32[256,128]{1,0:T(8,128)S(1)}, u32[]{:S(2)}, u32[]{:S(2)}) collective-permute-start(f32[256,128]{1,0:T(8,128)S(1)} %pad_maximum_fusion.rest_0_), channel_id=1, source_target_pairs={{0,64},{2,66},{4,68},{6,70},{8,72},{10,74},{12,76},{14,78},{16,208... | collective-permute-start | bytes 393224 | tf_op jit(solution)/shard_map/ppermute | solution.py:18
  24.5 10.0 %collective-permute-start.5 = (f32[256,128]{1,0:T(8,128)S(1)}, f32[256,128]{1,0:T(8,128)S(1)}, u32[]{:S(2)}, u32[]{:S(2)}) collective-permute-start(f32[256,128]{1,0:T(8,128)S(1)} %pad_maximum_fusion.rest_0_), channel_id=1, source_target_pairs={{0,32},{2,34},{4,36},{6,38},{8,40},{10,42},{12,44},{14,46},{16,18}... | collective-permute-start | bytes 393224 | tf_op jit(solution)/shard_map/ppermute | solution.py:18
  25.2 9.6 %collective-permute-start.10 = (f32[256,128]{1,0:T(8,128)S(1)}, f32[256,128]{1,0:T(8,128)S(1)}, u32[]{:S(2)}, u32[]{:S(2)}) collective-permute-start(f32[256,128]{1,0:T(8,128)S(1)} %collective-permute-done.4.rest_1_), channel_id=1, source_target_pairs={{0,64},{2,66},{4,68},{6,70},{8,72},{10,74},{12,76},{14,78},{16,208... | collective-permute-start | bytes 393224 | tf_op jit(solution)/shard_map/ppermute | solution.py:18
  27.1 8.6 %collective-permute-start.8 = (f32[256,128]{1,0:T(8,128)S(1)}, f32[256,128]{1,0:T(8,128)S(1)}, u32[]{:S(2)}, u32[]{:S(2)}) collective-permute-start(f32[256,128]{1,0:T(8,128)S(1)} %collective-permute-done.4.rest_1_), channel_id=1, source_target_pairs={{0,96},{2,98},{4,100},{6,102},{8,104},{10,106},{12,108},{14,110},{... | collective-permute-start | bytes 393224 | tf_op jit(solution)/shard_map/ppermute | solution.py:18
  28.4 9.8 %collective-permute-start.11 = (f32[256,128]{1,0:T(8,128)S(1)}, f32[256,128]{1,0:T(8,128)S(1)}, u32[]{:S(2)}, u32[]{:S(2)}) collective-permute-start(f32[256,128]{1,0:T(8,128)S(1)} %pad_maximum_fusion.rest_0_), channel_id=1, source_target_pairs={{0,16},{2,18},{4,20},{6,22},{8,24},{10,26},{12,28},{14,30},{16,0},... | collective-permute-start | bytes 393224 | tf_op jit(solution)/shard_map/ppermute | solution.py:18
  33.7 4.4 %collective-permute-start.9 = (f32[256,128]{1,0:T(8,128)S(1)}, f32[256,128]{1,0:T(8,128)S(1)}, u32[]{:S(2)}, u32[]{:S(2)}) collective-permute-start(f32[256,128]{1,0:T(8,128)S(1)} %collective-permute-done.4.rest_1_), channel_id=1, source_target_pairs={{0,32},{2,34},{4,36},{6,38},{8,40},{10,42},{12,44},{14,46},{16,18}... | collective-permute-start | bytes 393224 | tf_op jit(solution)/shard_map/ppermute | solution.py:18
  34.5 4.8 %collective-permute-start.12 = (f32[256,128]{1,0:T(8,128)S(1)}, f32[256,128]{1,0:T(8,128)S(1)}, u32[]{:S(2)}, u32[]{:S(2)}) collective-permute-start(f32[256,128]{1,0:T(8,128)S(1)} %collective-permute-done.4.rest_1_), channel_id=1, source_target_pairs={{0,16},{2,18},{4,20},{6,22},{8,24},{10,26},{12,28},{14,30},{16,0},... | collective-permute-start | bytes 393224 | tf_op jit(solution)/shard_map/ppermute | solution.py:18
  34.8 4.5 %collective-permute-start.16 = (f32[256,128]{1,0:T(8,128)S(1)}, f32[256,128]{1,0:T(8,128)S(1)}, u32[]{:S(2)}, u32[]{:S(2)}) collective-permute-start(f32[256,128]{1,0:T(8,128)S(1)} %collective-permute-done.10.rest_5_), channel_id=1, source_target_pairs={{0,16},{2,18},{4,20},{6,22},{8,24},{10,26},{12,28},{14,30},{16,0},... | collective-permute-start | bytes 393224 | tf_op jit(solution)/shard_map/ppermute | solution.py:18
  35.8 4.6 %collective-permute-start.13 = (f32[256,128]{1,0:T(8,128)S(1)}, f32[256,128]{1,0:T(8,128)S(1)}, u32[]{:S(2)}, u32[]{:S(2)}) collective-permute-start(f32[256,128]{1,0:T(8,128)S(1)} %collective-permute-done.5.rest_2_), channel_id=1, source_target_pairs={{0,16},{2,18},{4,20},{6,22},{8,24},{10,26},{12,28},{14,30},{16,0},... | collective-permute-start | bytes 393224 | tf_op jit(solution)/shard_map/ppermute | solution.py:18
  38.2 2.1 %collective-permute-start.15 = (f32[256,128]{1,0:T(8,128)S(1)}, f32[256,128]{1,0:T(8,128)S(1)}, u32[]{:S(2)}, u32[]{:S(2)}) collective-permute-start(f32[256,128]{1,0:T(8,128)S(1)} %collective-permute-done.6.rest_4_), channel_id=1, source_target_pairs={{0,16},{2,18},{4,20},{6,22},{8,24},{10,26},{12,28},{14,30},{16,0},... | collective-permute-start | bytes 393224 | tf_op jit(solution)/shard_map/ppermute | solution.py:18
  38.2 2.1 %collective-permute-start.14 = (f32[256,128]{1,0:T(8,128)S(1)}, f32[256,128]{1,0:T(8,128)S(1)}, u32[]{:S(2)}, u32[]{:S(2)}) collective-permute-start(f32[256,128]{1,0:T(8,128)S(1)} %collective-permute-done.9.rest_3_), channel_id=1, source_target_pairs={{0,16},{2,18},{4,20},{6,22},{8,24},{10,26},{12,28},{14,30},{16,0},... | collective-permute-start | bytes 393224 | tf_op jit(solution)/shard_map/ppermute | solution.py:18
  39.3 1.3 %collective-permute-start.17 = (f32[256,128]{1,0:T(8,128)S(1)}, f32[256,128]{1,0:T(8,128)S(1)}, u32[]{:S(2)}, u32[]{:S(2)}) collective-permute-start(f32[256,128]{1,0:T(8,128)S(1)} %collective-permute-done.7.rest_6_), channel_id=1, source_target_pairs={{0,16},{2,18},{4,20},{6,22},{8,24},{10,26},{12,28},{14,30},{16,0},... | collective-permute-start | bytes 393224 | tf_op jit(solution)/shard_map/ppermute | solution.py:18
  39.3 1.5 %collective-permute-start.18 = (f32[256,128]{1,0:T(8,128)S(1)}, f32[256,128]{1,0:T(8,128)S(1)}, u32[]{:S(2)}, u32[]{:S(2)}) collective-permute-start(f32[256,128]{1,0:T(8,128)S(1)} %collective-permute-done.8.rest_7_), channel_id=1, source_target_pairs={{0,16},{2,18},{4,20},{6,22},{8,24},{10,26},{12,28},{14,30},{16,0},... | collective-permute-start | bytes 393224 | tf_op jit(solution)/shard_map/ppermute | solution.py:18

commit v6 on v5

--- a/solution.py
+++ b/solution.py
@@ -150,6 +150,7 @@
     early = [trade(block, masks) for masks in (a, b, both)]
     late = [trade(later, masks) for masks in (a, b, both)]
     *early, late[2] = lax.optimization_barrier((*early, late[2]))
+    block, late[0] = lax.optimization_barrier((block, late[0]))
     pieces = [block, later] + [piece for pair in zip(early, late) for piece in pair]
     pieces += [trade(piece, (CORE, CORE)) for piece in pieces]
     return ladder(labels, integrals, pieces)

time: 49 us -> 51.7 us (1.055)
  starting transfers between devices: 31.2 us -> 33.9 us
    ppermute x18, starting transfers between devices: 27.6 us -> 30.3 us  [trade(): lax.ppermute(block, ('aa', 'ba'), [(i, j) for i, j in route if i != j])]
  transfers between devices with their start and end apart: 19 -> 19, of which waited for: 6 -> 7; matrix products, arithmetic and copies ran while one was open for 5% -> 4% of each run, Pallas kernels for 0% -> 0%
where the time goes in v6:
time: 51.7 us; the launch traced here: 51.3 us
  starting transfers between devices  33.9 us (66%)
  Pallas kernels  7.7 us (15%)
  waiting for transfers between devices  7.25 us (14%)
  other arithmetic  1.49 us (3%)
  local copies, waits for them, and re-layouts  0.9 us (2%)
    ppermute x18, starting transfers between devices, trade(): lax.ppermute(block, ('aa', 'ba'), [(i, j) for i, j in route if i != j])  30.3 us
    pallas_call x1, Pallas kernels, ladder(): pl.pallas_call(ladder_kernel, out_shape=jax.ShapeDtypeStruct((rows, 256),...  7.7 us
    ppermute x18, waiting for transfers between devices, trade(): lax.ppermute(block, ('aa', 'ba'), [(i, j) for i, j in route if i != j])  7.25 us
    ppermute x1, starting transfers between devices, trade_raw(): lax.ppermute(amplitudes, ('aa', 'ba', 'ao'), [(i, j) for i, j in route if...  3.57 us
  transfers between devices with their start and end apart: 19, of which 7 were waited for; matrix products, arithmetic and copies ran while one was open for 4% of the time, Pallas kernels for 0%

profile of v6, /device:TPU:1, one launch (start us, length us, event | category | flops | bytes accessed | tf_op | source)
XLA Modules:
  0.0 51.3 jit_solution(5024184179320776664)
XLA Ops:
  0.0 3.6 %collective-permute-start = (f32[16,256]{1,0:T(8,128)}, f32[16,256]{1,0:T(8,128)S(1)}, u32[]{:S(2)}, u32[]{:S(2)}) collective-permute-start(f32[16,256]{1,0:T(8,128)} %param.6), channel_id=1, source_target_pairs={{0,1},{1,0},{2,3},{3,2},{4,5},{5,4},{6,7},{7,6},{8,9},{9,8},{10,11... | collective-permute-start | bytes 49160 | tf_op jit(solution)/shard_map/ppermute | solution.py:23
  3.6 0.8 %broadcast_multiply_fusion = f32[16,256]{1,0:T(8,128)S(1)} fusion(f32[16,256]{1,0:T(8,128)} %param.6, f32[]{:T(128)S(6)} %convert_element_type.3), kind=kLoop, calls=%fused_computation.11 | loop fusion | flops 4096 | bytes 32772 | tf_op jit(solution)/shard_map/mul | solution.py:143
  4.3 0.7 %multiply_add_fusion = s32[2048]{0:T(1024)S(1)} fusion(s32[2048]{0:T(1024)} %param.9, s32[]{:T(128)S(6)} %add.9), kind=kLoop, calls=%fused_computation.3 | loop fusion | flops 94208 | bytes 16388 | tf_op jit(solution)/shard_map/add | solution.py:139
  5.0 0.7 %concatenate.12.labels = s32[2128]{0:T(1024)S(1)} concatenate(s32[2048]{0:T(1024)S(1)} %multiply_add_fusion, s32[64]{0:T(128)} %param.7, s32[16]{0:T(128)} %param.8), dimensions={0} | concatenate | bytes 17024 | tf_op jit(solution)/shard_map/concatenate | solution.py:139
  5.8 0.0 collective-permute-done
  5.8 0.1 rev.3
  6.0 6.1 %collective-permute-start.1 = (f32[32,128]{1,0:T(8,128)S(1)}, f32[32,128]{1,0:T(8,128)S(1)}, u32[]{:S(2)}, u32[]{:S(2)}) collective-permute-start(f32[32,128]{1,0:T(8,128)S(1)} %reshape.3), channel_id=1, source_target_pairs={{0,12},{2,14},{4,8},{6,10},{8,4},{10,6},{12,0},{14,2},{16,28},{18,... | collective-permute-start | bytes 49160 | tf_op jit(solution)/shard_map/ppermute | solution.py:18
  12.1 1.1 %collective-permute-done.1 = f32[32,128]{1,0:T(8,128)S(1)} collective-permute-done((f32[32,128]{1,0:T(8,128)S(1)}, f32[32,128]{1,0:T(8,128)S(1)}, u32[]{:S(2)}, u32[]{:S(2)}) %collective-permute-start.1) | collective-permute-done | bytes 16416 | tf_op jit(solution)/shard_map/ppermute | solution.py:18
  13.2 1.2 %collective-permute-start.2 = (f32[64,128]{1,0:T(8,128)S(1)}, f32[64,128]{1,0:T(8,128)S(1)}, u32[]{:S(2)}, u32[]{:S(2)}) collective-permute-start(f32[64,128]{1,0:T(8,128)S(1)} %pad_maximum_fusion.2), channel_id=1, source_target_pairs={{0,4},{2,6},{4,0},{6,2},{8,12},{10,14},{12,8},{14,10},{16,20},{18,... | collective-permute-start | bytes 98312 | tf_op jit(solution)/shard_map/ppermute | solution.py:18
  14.4 2.5 %collective-permute-done.2 = f32[64,128]{1,0:T(8,128)S(1)} collective-permute-done((f32[64,128]{1,0:T(8,128)S(1)}, f32[64,128]{1,0:T(8,128)S(1)}, u32[]{:S(2)}, u32[]{:S(2)}) %collective-permute-start.2) | collective-permute-done | bytes 32800 | tf_op jit(solution)/shard_map/ppermute | solution.py:18
  16.9 0.5 %collective-permute-start.3 = (f32[128,128]{1,0:T(8,128)S(1)}, f32[128,128]{1,0:T(8,128)S(1)}, u32[]{:S(2)}, u32[]{:S(2)}) collective-permute-start(f32[128,128]{1,0:T(8,128)S(1)} %pad_maximum_fusion.1), channel_id=1, source_target_pairs={{0,192},{2,194},{4,196},{6,198},{8,200},{10,202},{12,204},{14,206}... | collective-permute-start | bytes 196616 | tf_op jit(solution)/shard_map/ppermute | solution.py:18
  17.4 2.6 %collective-permute-done.3 = f32[128,128]{1,0:T(8,128)S(1)} collective-permute-done((f32[128,128]{1,0:T(8,128)S(1)}, f32[128,128]{1,0:T(8,128)S(1)}, u32[]{:S(2)}, u32[]{:S(2)}) %collective-permute-start.3) | collective-permute-done | bytes 65568 | tf_op jit(solution)/shard_map/ppermute | solution.py:18
  20.0 1.4 %collective-permute-start.4 = (f32[256,128]{1,0:T(8,128)S(1)}, f32[256,128]{1,0:T(8,128)S(1)}, u32[]{:S(2)}, u32[]{:S(2)}) collective-permute-start(f32[256,128]{1,0:T(8,128)S(1)} %pad_maximum_fusion.rest_0_), channel_id=1, source_target_pairs={{0,2},{2,0},{4,6},{6,4},{8,10},{10,8},{12,14},{14,12},{16,80},{18,... | collective-permute-start | bytes 393224 | tf_op jit(solution)/shard_map/ppermute | solution.py:18
  21.4 2.4 %collective-permute-start.8 = (f32[256,128]{1,0:T(8,128)S(1)}, f32[256,128]{1,0:T(8,128)S(1)}, u32[]{:S(2)}, u32[]{:S(2)}) collective-permute-start(f32[256,128]{1,0:T(8,128)S(1)} %pad_maximum_fusion.rest_0_), channel_id=1, source_target_pairs={{0,96},{2,98},{4,100},{6,102},{8,104},{10,106},{12,108},{14,110},{... | collective-permute-start | bytes 393224 | tf_op jit(solution)/shard_map/ppermute | solution.py:18
  23.7 0.8 %collective-permute-start.7 = (f32[256,128]{1,0:T(8,128)S(1)}, f32[256,128]{1,0:T(8,128)S(1)}, u32[]{:S(2)}, u32[]{:S(2)}) collective-permute-start(f32[256,128]{1,0:T(8,128)S(1)} %pad_maximum_fusion.rest_0_), channel_id=1, source_target_pairs={{0,64},{2,66},{4,68},{6,70},{8,72},{10,74},{12,76},{14,78},{16,208... | collective-permute-start | bytes 393224 | tf_op jit(solution)/shard_map/ppermute | solution.py:18
  24.5 0.0 collective-permute-done.4.rest_1_
  24.5 2.1 %collective-permute-start.10 = (f32[256,128]{1,0:T(8,128)S(1)}, f32[256,128]{1,0:T(8,128)S(1)}, u32[]{:S(2)}, u32[]{:S(2)}) collective-permute-start(f32[256,128]{1,0:T(8,128)S(1)} %collective-permute-done.4.rest_1_), channel_id=1, source_target_pairs={{0,64},{2,66},{4,68},{6,70},{8,72},{10,74},{12,76},{14,78},{16,208... | collective-permute-start | bytes 393224 | tf_op jit(solution)/shard_map/ppermute | solution.py:18
  26.6 0.7 %collective-permute-start.6 = (f32[256,128]{1,0:T(8,128)S(1)}, f32[256,128]{1,0:T(8,128)S(1)}, u32[]{:S(2)}, u32[]{:S(2)}) collective-permute-start(f32[256,128]{1,0:T(8,128)S(1)} %pad_maximum_fusion.rest_0_), channel_id=1, source_target_pairs={{0,32},{2,34},{4,36},{6,38},{8,40},{10,42},{12,44},{14,46},{16,18}... | collective-permute-start | bytes 393224 | tf_op jit(solution)/shard_map/ppermute | solution.py:18
  27.4 1.0 %collective-permute-start.9 = (f32[256,128]{1,0:T(8,128)S(1)}, f32[256,128]{1,0:T(8,128)S(1)}, u32[]{:S(2)}, u32[]{:S(2)}) collective-permute-start(f32[256,128]{1,0:T(8,128)S(1)} %collective-permute-done.4.rest_1_), channel_id=1, source_target_pairs={{0,96},{2,98},{4,100},{6,102},{8,104},{10,106},{12,108},{14,110},{... | collective-permute-start | bytes 393224 | tf_op jit(solution)/shard_map/ppermute | solution.py:18
  28.4 0.0 collective-permute-done.8.rest_6_
  28.4 0.7 %collective-permute-start.5 = (f32[256,128]{1,0:T(8,128)S(1)}, f32[256,128]{1,0:T(8,128)S(1)}, u32[]{:S(2)}, u32[]{:S(2)}) collective-permute-start(f32[256,128]{1,0:T(8,128)S(1)} %collective-permute-done.4.rest_1_), channel_id=1, source_target_pairs={{0,32},{2,34},{4,36},{6,38},{8,40},{10,42},{12,44},{14,46},{16,18}... | collective-permute-start | bytes 393224 | tf_op jit(solution)/shard_map/ppermute | solution.py:18
  29.1 0.0 collective-permute-done.7.rest_4_
  29.1 7.7 %collective-permute-start.12 = (f32[256,128]{1,0:T(8,128)S(1)}, f32[256,128]{1,0:T(8,128)S(1)}, u32[]{:S(2)}, u32[]{:S(2)}) collective-permute-start(f32[256,128]{1,0:T(8,128)S(1)} %collective-permute-done.4.rest_1_), channel_id=1, source_target_pairs={{0,16},{2,18},{4,20},{6,22},{8,24},{10,26},{12,28},{14,30},{16,0},... | collective-permute-start | bytes 393224 | tf_op jit(solution)/shard_map/ppermute | solution.py:18
  36.8 0.0 collective-permute-done.10.rest_5_
  36.8 0.1 collective-permute-start.16
  36.9 0.0 collective-permute-done.6.rest_2_
  36.9 0.0 collective-permute-done.9.rest_7_
  36.9 4.3 %collective-permute-start.13 = (f32[256,128]{1,0:T(8,128)S(1)}, f32[256,128]{1,0:T(8,128)S(1)}, u32[]{:S(2)}, u32[]{:S(2)}) collective-permute-start(f32[256,128]{1,0:T(8,128)S(1)} %collective-permute-done.6.rest_2_), channel_id=1, source_target_pairs={{0,16},{2,18},{4,20},{6,22},{8,24},{10,26},{12,28},{14,30},{16,0},... | collective-permute-start | bytes 393224 | tf_op jit(solution)/shard_map/ppermute | solution.py:18
  41.2 0.0 collective-permute-start.15
  41.2 0.0 collective-permute-done.5.rest_3_
  41.2 0.5 collective-permute-start.17
  41.7 0.0 collective-permute-done.12.rest_9_
  41.7 0.1 collective-permute-start.18
  41.8 0.0 collective-permute-done.16.rest_13_
  41.8 0.4 collective-permute-start.11
  42.2 0.0 collective-permute-done.13.rest_10_
  42.2 0.3 collective-permute-start.14
  42.5 0.0 collective-permute-done.15.rest_12_
  42.5 0.2 collective-permute-done.17.rest_14_
  42.7 0.3 collective-permute-done.18.rest_15_
  43.0 0.2 collective-permute-done.11.rest_8_
  43.2 0.3 collective-permute-done.14.rest_11_
  43.6 7.7 %shard_map.55 = f32[8192,256]{1,0:T(8,128)} custom-call(s32[2128]{0:T(1024)S(1)} %concatenate.12.labels, f32[8192,256]{1,0:T(8,128)} %integrals.1, f32[256,128]{1,0:T(8,128)S(1)} %pad_maximum_fusion.rest_0_, f32[256,128]{1,0:T(8,128)S(1)} %collective-permute-done.4.rest_1_, f32[256,128]{1,0:T(8,128)S(1)} %collective-permute-done.6.rest_2_, ...), custom_call_target="tpu_custom_call" | custom-call | tf_op jit(solution)/shard_map/pallas_call | solution.py:111
  (5 shorter events, 0.0 us)
Async XLA Ops:
  0.0 5.8 %collective-permute-start = (f32[16,256]{1,0:T(8,128)}, f32[16,256]{1,0:T(8,128)S(1)}, u32[]{:S(2)}, u32[]{:S(2)}) collective-permute-start(f32[16,256]{1,0:T(8,128)} %param.6), channel_id=1, source_target_pairs={{0,1},{1,0},{2,3},{3,2},{4,5},{5,4},{6,7},{7,6},{8,9},{9,8},{10,11... | collective-permute-start | bytes 49160 | tf_op jit(solution)/shard_map/ppermute | solution.py:23
  6.0 7.2 %collective-permute-start.1 = (f32[32,128]{1,0:T(8,128)S(1)}, f32[32,128]{1,0:T(8,128)S(1)}, u32[]{:S(2)}, u32[]{:S(2)}) collective-permute-start(f32[32,128]{1,0:T(8,128)S(1)} %reshape.3), channel_id=1, source_target_pairs={{0,12},{2,14},{4,8},{6,10},{8,4},{10,6},{12,0},{14,2},{16,28},{18,... | collective-permute-start | bytes 49160 | tf_op jit(solution)/shard_map/ppermute | solution.py:18
  13.2 3.7 %collective-permute-start.2 = (f32[64,128]{1,0:T(8,128)S(1)}, f32[64,128]{1,0:T(8,128)S(1)}, u32[]{:S(2)}, u32[]{:S(2)}) collective-permute-start(f32[64,128]{1,0:T(8,128)S(1)} %pad_maximum_fusion.2), channel_id=1, source_target_pairs={{0,4},{2,6},{4,0},{6,2},{8,12},{10,14},{12,8},{14,10},{16,20},{18,... | collective-permute-start | bytes 98312 | tf_op jit(solution)/shard_map/ppermute | solution.py:18
  16.9 3.1 %collective-permute-start.3 = (f32[128,128]{1,0:T(8,128)S(1)}, f32[128,128]{1,0:T(8,128)S(1)}, u32[]{:S(2)}, u32[]{:S(2)}) collective-permute-start(f32[128,128]{1,0:T(8,128)S(1)} %pad_maximum_fusion.1), channel_id=1, source_target_pairs={{0,192},{2,194},{4,196},{6,198},{8,200},{10,202},{12,204},{14,206}... | collective-permute-start | bytes 196616 | tf_op jit(solution)/shard_map/ppermute | solution.py:18
  20.0 4.5 %collective-permute-start.4 = (f32[256,128]{1,0:T(8,128)S(1)}, f32[256,128]{1,0:T(8,128)S(1)}, u32[]{:S(2)}, u32[]{:S(2)}) collective-permute-start(f32[256,128]{1,0:T(8,128)S(1)} %pad_maximum_fusion.rest_0_), channel_id=1, source_target_pairs={{0,2},{2,0},{4,6},{6,4},{8,10},{10,8},{12,14},{14,12},{16,80},{18,... | collective-permute-start | bytes 393224 | tf_op jit(solution)/shard_map/ppermute | solution.py:18
  21.4 7.0 %collective-permute-start.8 = (f32[256,128]{1,0:T(8,128)S(1)}, f32[256,128]{1,0:T(8,128)S(1)}, u32[]{:S(2)}, u32[]{:S(2)}) collective-permute-start(f32[256,128]{1,0:T(8,128)S(1)} %pad_maximum_fusion.rest_0_), channel_id=1, source_target_pairs={{0,96},{2,98},{4,100},{6,102},{8,104},{10,106},{12,108},{14,110},{... | collective-permute-start | bytes 393224 | tf_op jit(solution)/shard_map/ppermute | solution.py:18
  23.7 5.4 %collective-permute-start.7 = (f32[256,128]{1,0:T(8,128)S(1)}, f32[256,128]{1,0:T(8,128)S(1)}, u32[]{:S(2)}, u32[]{:S(2)}) collective-permute-start(f32[256,128]{1,0:T(8,128)S(1)} %pad_maximum_fusion.rest_0_), channel_id=1, source_target_pairs={{0,64},{2,66},{4,68},{6,70},{8,72},{10,74},{12,76},{14,78},{16,208... | collective-permute-start | bytes 393224 | tf_op jit(solution)/shard_map/ppermute | solution.py:18
  24.5 12.3 %collective-permute-start.10 = (f32[256,128]{1,0:T(8,128)S(1)}, f32[256,128]{1,0:T(8,128)S(1)}, u32[]{:S(2)}, u32[]{:S(2)}) collective-permute-start(f32[256,128]{1,0:T(8,128)S(1)} %collective-permute-done.4.rest_1_), channel_id=1, source_target_pairs={{0,64},{2,66},{4,68},{6,70},{8,72},{10,74},{12,76},{14,78},{16,208... | collective-permute-start | bytes 393224 | tf_op jit(solution)/shard_map/ppermute | solution.py:18
  26.6 10.3 %collective-permute-start.6 = (f32[256,128]{1,0:T(8,128)S(1)}, f32[256,128]{1,0:T(8,128)S(1)}, u32[]{:S(2)}, u32[]{:S(2)}) collective-permute-start(f32[256,128]{1,0:T(8,128)S(1)} %pad_maximum_fusion.rest_0_), channel_id=1, source_target_pairs={{0,32},{2,34},{4,36},{6,38},{8,40},{10,42},{12,44},{14,46},{16,18}... | collective-permute-start | bytes 393224 | tf_op jit(solution)/shard_map/ppermute | solution.py:18
  27.4 9.5 %collective-permute-start.9 = (f32[256,128]{1,0:T(8,128)S(1)}, f32[256,128]{1,0:T(8,128)S(1)}, u32[]{:S(2)}, u32[]{:S(2)}) collective-permute-start(f32[256,128]{1,0:T(8,128)S(1)} %collective-permute-done.4.rest_1_), channel_id=1, source_target_pairs={{0,96},{2,98},{4,100},{6,102},{8,104},{10,106},{12,108},{14,110},{... | collective-permute-start | bytes 393224 | tf_op jit(solution)/shard_map/ppermute | solution.py:18
  28.4 12.8 %collective-permute-start.5 = (f32[256,128]{1,0:T(8,128)S(1)}, f32[256,128]{1,0:T(8,128)S(1)}, u32[]{:S(2)}, u32[]{:S(2)}) collective-permute-start(f32[256,128]{1,0:T(8,128)S(1)} %collective-permute-done.4.rest_1_), channel_id=1, source_target_pairs={{0,32},{2,34},{4,36},{6,38},{8,40},{10,42},{12,44},{14,46},{16,18}... | collective-permute-start | bytes 393224 | tf_op jit(solution)/shard_map/ppermute | solution.py:18
  29.1 12.6 %collective-permute-start.12 = (f32[256,128]{1,0:T(8,128)S(1)}, f32[256,128]{1,0:T(8,128)S(1)}, u32[]{:S(2)}, u32[]{:S(2)}) collective-permute-start(f32[256,128]{1,0:T(8,128)S(1)} %collective-permute-done.4.rest_1_), channel_id=1, source_target_pairs={{0,16},{2,18},{4,20},{6,22},{8,24},{10,26},{12,28},{14,30},{16,0},... | collective-permute-start | bytes 393224 | tf_op jit(solution)/shard_map/ppermute | solution.py:18
  36.8 5.0 %collective-permute-start.16 = (f32[256,128]{1,0:T(8,128)S(1)}, f32[256,128]{1,0:T(8,128)S(1)}, u32[]{:S(2)}, u32[]{:S(2)}) collective-permute-start(f32[256,128]{1,0:T(8,128)S(1)} %collective-permute-done.10.rest_5_), channel_id=1, source_target_pairs={{0,16},{2,18},{4,20},{6,22},{8,24},{10,26},{12,28},{14,30},{16,0},... | collective-permute-start | bytes 393224 | tf_op jit(solution)/shard_map/ppermute | solution.py:18
  36.9 5.3 %collective-permute-start.13 = (f32[256,128]{1,0:T(8,128)S(1)}, f32[256,128]{1,0:T(8,128)S(1)}, u32[]{:S(2)}, u32[]{:S(2)}) collective-permute-start(f32[256,128]{1,0:T(8,128)S(1)} %collective-permute-done.6.rest_2_), channel_id=1, source_target_pairs={{0,16},{2,18},{4,20},{6,22},{8,24},{10,26},{12,28},{14,30},{16,0},... | collective-permute-start | bytes 393224 | tf_op jit(solution)/shard_map/ppermute | solution.py:18
  41.2 1.4 %collective-permute-start.15 = (f32[256,128]{1,0:T(8,128)S(1)}, f32[256,128]{1,0:T(8,128)S(1)}, u32[]{:S(2)}, u32[]{:S(2)}) collective-permute-start(f32[256,128]{1,0:T(8,128)S(1)} %collective-permute-done.7.rest_4_), channel_id=1, source_target_pairs={{0,16},{2,18},{4,20},{6,22},{8,24},{10,26},{12,28},{14,30},{16,0},... | collective-permute-start | bytes 393224 | tf_op jit(solution)/shard_map/ppermute | solution.py:18
  41.2 1.5 %collective-permute-start.17 = (f32[256,128]{1,0:T(8,128)S(1)}, f32[256,128]{1,0:T(8,128)S(1)}, u32[]{:S(2)}, u32[]{:S(2)}) collective-permute-start(f32[256,128]{1,0:T(8,128)S(1)} %collective-permute-done.8.rest_6_), channel_id=1, source_target_pairs={{0,16},{2,18},{4,20},{6,22},{8,24},{10,26},{12,28},{14,30},{16,0},... | collective-permute-start | bytes 393224 | tf_op jit(solution)/shard_map/ppermute | solution.py:18
  41.7 1.3 %collective-permute-start.18 = (f32[256,128]{1,0:T(8,128)S(1)}, f32[256,128]{1,0:T(8,128)S(1)}, u32[]{:S(2)}, u32[]{:S(2)}) collective-permute-start(f32[256,128]{1,0:T(8,128)S(1)} %collective-permute-done.9.rest_7_), channel_id=1, source_target_pairs={{0,16},{2,18},{4,20},{6,22},{8,24},{10,26},{12,28},{14,30},{16,0},... | collective-permute-start | bytes 393224 | tf_op jit(solution)/shard_map/ppermute | solution.py:18
  41.8 1.4 %collective-permute-start.11 = (f32[256,128]{1,0:T(8,128)S(1)}, f32[256,128]{1,0:T(8,128)S(1)}, u32[]{:S(2)}, u32[]{:S(2)}) collective-permute-start(f32[256,128]{1,0:T(8,128)S(1)} %pad_maximum_fusion.rest_0_), channel_id=1, source_target_pairs={{0,16},{2,18},{4,20},{6,22},{8,24},{10,26},{12,28},{14,30},{16,0},... | collective-permute-start | bytes 393224 | tf_op jit(solution)/shard_map/ppermute | solution.py:18
  42.2 1.3 %collective-permute-start.14 = (f32[256,128]{1,0:T(8,128)S(1)}, f32[256,128]{1,0:T(8,128)S(1)}, u32[]{:S(2)}, u32[]{:S(2)}) collective-permute-start(f32[256,128]{1,0:T(8,128)S(1)} %collective-permute-done.5.rest_3_), channel_id=1, source_target_pairs={{0,16},{2,18},{4,20},{6,22},{8,24},{10,26},{12,28},{14,30},{16,0},... | collective-permute-start | bytes 393224 | tf_op jit(solution)/shard_map/ppermute | solution.py:18
